TPU v7x, 32 devices: a whole 2x2x4 slice. The times are simulated.
32 devices in a mesh: span: 2 (over x), brick: 16 (over z, y, core).
Axes of the slice: x: 2, y: 2, z: 4, core: 2. Of those that a mesh axis runs over, the one named last changes fastest.
Arguments:
- measured: bfloat16 [4, 1024, 32, 128], P(None, ('span', 'brick')), parts along dimension 1, may hold values from 0.175 to 201.6, as said below
- psf: float32 [4, 3, 31], replicated, may hold values from 0.05 to 1
- stem_params: float32 [2, 16], replicated, may hold values from -4 to 4
- conv_weight: bfloat16 [432, 16], replicated, may hold values from -0.3125 to 0.3125
- head_params: float32 [2, 16], replicated, may hold values from -3 to 3
Outputs:
- estimate: float32 [1024, 32, 128], P(('span', 'brick')), parts along dimension 0
- logits: float32 [1024, 32, 128], P(('span', 'brick')), parts along dimension 0
There are 2 independent parts, one for each index of `span`. A program takes and returns all parts, laid end to end along the dimension named above; an argument that names none is the same for every part. Nothing has to cross between parts.
Inputs may be any that keep to these rules, and one draw needn't show every extreme that they name: `measured`: positive.
All inputs are finite; a program needn't handle non-finite values.
Results may differ from a plain program's by a relative error of at most 0.0049.
Values may be sent and summed in bfloat16 or wider, within the bound.
No kernel may reach another device: no remote copies, remote signals or barrier semaphores. Data moves between devices by JAX's collectives and lax.ppermute only.
A program may use at most 128 MiB of HBM per device.

v0:
```python
import functools
import jax, jax.numpy as jnp
from jax import lax
from jax.experimental import pallas as pl
from jax.experimental.pallas import tpu as pltpu
from jax.sharding import PartitionSpec as P

F32, BF16 = jnp.float32, jnp.bfloat16
HALO = 16
SMEM = pl.BlockSpec(memory_space=pltpu.SMEM)
VMEM = pl.BlockSpec(memory_space=pltpu.VMEM)


def iotas(shape):
    return lax.broadcasted_iota(jnp.int32, shape, 0), lax.broadcasted_iota(jnp.int32, shape, 1)


def bands(k_ref, dim, index):
    views, taps = k_ref.shape[0], k_ref.shape[2]
    out = [jnp.zeros(index.shape, F32)] * views
    for t in range(taps):
        hit = index == t
        out = [jnp.where(hit, k_ref[v, dim, t], out[v]) for v in range(views)]
    return out


def prep_kernel(k_ref, meas_ref, kx_ref, bz_ref, bzt_ref, ly_ref, lyt_ref, bxt_ref, bxt2_ref, meast_ref, est_ref, nat_ref):
    views = k_ref.shape[0]
    reach = (k_ref.shape[2] - 1) // 2
    r, c = iotas((64, 96))
    for v, m in enumerate(bands(k_ref, 0, c - r - HALO + reach)):
        kx_ref[v * 64:(v + 1) * 64, :] = m.astype(BF16)
    for ref, rows, first in ((bxt_ref, 32, 0), (bxt2_ref, 48, -8)):
        r, c = iotas((rows, 512))
        for v, m in enumerate(bands(k_ref, 0, (r + first) - ((c & 63) - HALO) + reach)):
            ref[v * rows:(v + 1) * rows, :] = jnp.where(((c >> 6) & 3) == v, m, 0.0).astype(BF16)
    r, c = iotas((128, 128))
    zero = jnp.zeros((128, 128), BF16)
    for ref, sign in ((bz_ref, 1), (bzt_ref, -1)):
        for v, m in enumerate(bands(k_ref, 2, sign * (r - c) + reach)):
            p, a = v // 2, v % 2
            ref[p, a * 128:(a + 1) * 128, a * 128:(a + 1) * 128] = m.astype(BF16)
            ref[p, a * 128:(a + 1) * 128, (1 - a) * 128:(2 - a) * 128] = zero
    r, c = iotas((32, 32))
    er, ec = iotas((256, 32))
    spread = ((er >> 3) == ec).astype(F32).astype(BF16)
    tr, tc = iotas((32, 256))
    spread_t = ((tc >> 3) == tr).astype(F32).astype(BF16)
    fr, fc = iotas((256, 256))
    same = (fr & 7) == (fc & 7)
    for ref, sign in ((ly_ref, 1), (lyt_ref, -1)):
        for v, m in enumerate(bands(k_ref, 1, sign * (c - r) + reach)):
            wide = jnp.dot(spread, m.astype(BF16), preferred_element_type=F32).astype(BF16)
            full = jnp.dot(wide, spread_t, preferred_element_type=F32)
            ref[v] = jnp.where(same, full, 0.0).astype(BF16)
    for v in range(views):
        nat_ref[v] = meas_ref[v].astype(F32)

    def turn(y, _):
        acc = None
        for v in range(views):
            m = nat_ref[v, pl.ds(y, 32, stride=32), :]
            acc = m if acc is None else acc + m
            meast_ref[v, y] = m.astype(BF16)
        est_ref[y] = acc * (1.0 / views)
        return 0

    lax.fori_loop(0, 32, turn, 0)


def prep_call(kernels, measured):
    views = measured.shape[0]
    out = [
        ((views * 64, 96), BF16),
        ((2, 256, 256), BF16),
        ((2, 256, 256), BF16),
        ((views, 256, 256), BF16),
        ((views, 256, 256), BF16),
        ((views * 32, 512), BF16),
        ((views * 48, 512), BF16),
        ((views, 32, 32, 128), BF16),
        ((32, 32, 128), F32),
    ]
    return pl.pallas_call(
        prep_kernel,
        out_shape=[jax.ShapeDtypeStruct(s, d) for s, d in out],
        in_specs=[SMEM, VMEM],
        out_specs=[VMEM] * len(out),
        scratch_shapes=[pltpu.VMEM((views, 1024, 128), F32)],
        compiler_params=pltpu.CompilerParams(vmem_limit_bytes=40 * 2**20),
        cost_estimate=pl.CostEstimate(flops=10**9, bytes_accessed=20 * 10**6, transcendentals=0),
        name="bands_and_turn",
    )(kernels, measured.reshape(views, 1024, 128))


def correct(eb_ref, meas, kx_ref, bz_ref, bzt_ref, ly_ref, lyt_ref, bxt_ref, rows, a_ref, b_ref, d_ref, finish):
    def ahead_x(i, _):
        y = i * 2
        both = jnp.concatenate([eb_ref[y], eb_ref[y + 1]], axis=1)
        p = jnp.dot(kx_ref[...], both, preferred_element_type=F32).astype(BF16)
        for v in range(4):
            a_ref[v, y] = p[v * 64:(v + 1) * 64, :128]
            a_ref[v, y + 1] = p[v * 64:(v + 1) * 64, 128:]
        return 0

    lax.fori_loop(0, 16, ahead_x, 0, unroll=2)

    def along_z(i, _):
        y = i * 4
        for p in range(2):
            both = jnp.concatenate([a_ref[2 * p + a, pl.ds(y, 4)].reshape(256, 128) for a in range(2)], axis=1)
            q = jnp.dot(both, bz_ref[p], preferred_element_type=F32)
            for a in range(2):
                b_ref[2 * p + a, pl.ds(y, 4)] = q[:, a * 128:(a + 1) * 128].reshape(4, 64, 128)
        return 0

    lax.fori_loop(0, 8, along_z, 0, unroll=2)

    for v in range(4):
        for k in range(4):
            x = k * 16
            halves = [b_ref[v, :, x + 8 * a:x + 8 * a + 8, :].reshape(256, 128).astype(BF16) for a in range(2)]
            q = jnp.dot(ly_ref[v], jnp.concatenate(halves, axis=1), preferred_element_type=F32)
            m = meas[v, :, x:x + 16, :].astype(F32)
            halves = []
            for a in range(2):
                top = m[:, 8 * a:8 * a + 8, :].reshape(256, 128)
                ratio = jnp.where(top > 0.0, top / q[:, a * 128:(a + 1) * 128], 0.0)
                halves.append(ratio.astype(BF16))
            q = jnp.dot(lyt_ref[v], jnp.concatenate(halves, axis=1), preferred_element_type=F32)
            halves = [q[:, a * 128:(a + 1) * 128].reshape(32, 8, 128) for a in range(2)]
            a_ref[v, :, x:x + 16, :] = jnp.concatenate(halves, axis=1).astype(BF16)

    def back_z(i, _):
        y = i * 4
        for p in range(2):
            both = jnp.concatenate([a_ref[2 * p + a, pl.ds(y, 4)].reshape(256, 128) for a in range(2)], axis=1)
            q = jnp.dot(both, bzt_ref[p], preferred_element_type=F32)
            for a in range(2):
                w = q[:, a * 128:(a + 1) * 128].reshape(4, 64, 128)
                hi = w.astype(BF16)
                at = (2 * p + a) * 64
                d_ref[pl.ds(y, 4), at:at + 64, :] = hi
                d_ref[pl.ds(y, 4), 256 + at:256 + at + 64, :] = (w - hi.astype(F32)).astype(BF16)
        return 0

    lax.fori_loop(0, 8, back_z, 0, unroll=2)

    def back_x(i, carry):
        y = i * 2
        both = jnp.concatenate([d_ref[y], d_ref[y + 1]], axis=1)
        p = jnp.dot(bxt_ref[...], both, preferred_element_type=F32)
        f = p[:rows]
        for v in range(1, 4):
            f = f * p[v * rows:(v + 1) * rows]
        carry = finish(y, f[:, :128], carry)
        return finish(y + 1, f[:, 128:], carry)

    return lax.fori_loop(0, 16, back_x, jnp.zeros((8, 128), F32), unroll=2)


def first_kernel(lo_ref, hi_ref, meast_ref, est_ref, kx, bz, bzt, ly, lyt, bxt, new_ref, newb_ref, measx_ref,
                 nat_ref, eb_ref, a_ref, b_ref, d_ref):
    for side, ref in enumerate((lo_ref, hi_ref)):
        for v in range(5):
            nat_ref[side, v] = ref[v].astype(F32)

    def turn(y, _):
        for side, near, far, at in ((0, 16, 0, 0), (1, 64, 80, 48)):
            acc = None
            for v in range(4):
                m = nat_ref[side, v, pl.ds(y, 16, stride=32), :]
                acc = m if acc is None else acc + m
                measx_ref[v, y, at:at + 16, :] = m.astype(BF16)
            eb_ref[y, near:near + 16, :] = (acc * 0.25).astype(BF16)
            eb_ref[y, far:far + 16, :] = nat_ref[side, 4, pl.ds(y, 16, stride=32), :].astype(BF16)
        for v in range(4):
            measx_ref[v, y, 16:48, :] = meast_ref[v, y]
        eb_ref[y, 32:64, :] = est_ref[y].astype(BF16)
        return 0

    lax.fori_loop(0, 32, turn, 0, unroll=2)

    def finish(y, f, carry):
        e = est_ref[y] * f
        new_ref[y] = e
        newb_ref[y] = e.astype(BF16)
        return carry

    correct(eb_ref, measx_ref, kx, bz, bzt, ly, lyt, bxt, 32, a_ref, b_ref, d_ref, finish)


def second_kernel(lo_ref, hi_ref, measx_ref, est_ref, kx, bz, bzt, ly, lyt, bxt, out_ref, ext_ref, sum_ref,
                  eb_ref, a_ref, b_ref, d_ref):
    def fill(y, _):
        eb_ref[y, 0:32, :] = lo_ref[y]
        eb_ref[y, 32:64, :] = est_ref[y].astype(BF16)
        eb_ref[y, 64:96, :] = hi_ref[y]
        return 0

    lax.fori_loop(0, 32, fill, 0, unroll=2)

    def finish(y, f, carry):
        mid = est_ref[y] * f[8:40]
        before = lo_ref[y, 16:32, :].astype(F32)[8:16] * f[0:8]
        after = hi_ref[y, 0:16, :].astype(F32)[0:8] * f[40:48]
        out_ref[pl.ds(y, 32, stride=32), :] = mid
        ext_ref[pl.ds(32 + y, 32, stride=32), :] = mid
        ext_ref[pl.ds(y, 1), :] = before[7:8]
        ext_ref[pl.ds(33 * 32 + y, 1), :] = after[0:1]
        return carry + ((mid[0:8] + mid[8:16]) + (mid[16:24] + mid[24:32]))

    total = correct(eb_ref, measx_ref, kx, bz, bzt, ly, lyt, bxt, 48, a_ref, b_ref, d_ref, finish)
    whole = jnp.sum(total)
    for k in range(sum_ref.shape[0]):
        sum_ref[k] = whole


SCRATCH = [
    pltpu.VMEM((32, 96, 128), BF16),
    pltpu.VMEM((4, 32, 64, 128), BF16),
    pltpu.VMEM((4, 32, 64, 128), F32),
    pltpu.VMEM((32, 512, 128), BF16),
]
COST = pl.CostEstimate(flops=6 * 10**9, bytes_accessed=8 * 10**6, transcendentals=0)


def first_call(lo, hi, meast, est, mats):
    return pl.pallas_call(
        first_kernel,
        out_shape=[
            jax.ShapeDtypeStruct((32, 32, 128), F32),
            jax.ShapeDtypeStruct((32, 32, 128), BF16),
            jax.ShapeDtypeStruct((4, 32, 64, 128), BF16),
        ],
        in_specs=[VMEM] * 10,
        out_specs=[VMEM] * 3,
        scratch_shapes=[pltpu.VMEM((2, 5, 512, 128), F32)] + SCRATCH,
        compiler_params=pltpu.CompilerParams(vmem_limit_bytes=48 * 2**20),
        cost_estimate=COST,
        name="first_iteration",
    )(lo.reshape(5, 512, 128), hi.reshape(5, 512, 128), meast, est, *mats)


def second_call(lo, hi, measx, est, mats, bricks):
    return pl.pallas_call(
        second_kernel,
        out_shape=[
            jax.ShapeDtypeStruct((1024, 128), F32),
            jax.ShapeDtypeStruct((34 * 32, 128), F32),
            jax.ShapeDtypeStruct((bricks,), F32),
        ],
        in_specs=[VMEM] * 10,
        out_specs=[VMEM, VMEM, SMEM],
        scratch_shapes=SCRATCH,
        compiler_params=pltpu.CompilerParams(vmem_limit_bytes=48 * 2**20),
        cost_estimate=COST,
        name="second_iteration",
    )(lo, hi, measx, est, *mats)

YB = 8


def conv_matrix(conv_weight, yb=YB):
    ch = conv_weight.shape[1]
    w = conv_weight.reshape(3, 3, 3, ch, ch)
    rows = []
    for yo in range(yb):
        rows.append(jnp.pad(w, ((0, 0), (yo, yb - 1 - yo), (0, 0), (0, 0), (0, 0))))
    m = jnp.stack(rows, 0)
    m = m.transpose(1, 5, 0, 2, 3, 4)
    return m.reshape(3 * ch * yb, (yb + 2) * 3 * ch)


def conv_kernel(yb, count, tot_ref, flag_ref, head_ref, est_ref, stem_ref, w_ref, out_ref, n_ref, f_ref, c_ref):
    planes = est_ref.shape[0] // 32
    ch = stem_ref.shape[1]
    total = tot_ref[0]
    for k in range(1, tot_ref.shape[0]):
        total = total + tot_ref[k]
    scale = count / jnp.full((8, 128), total, jnp.float32)
    lane = lax.broadcasted_iota(jnp.int32, (ch, 128), 1)
    w0, b0 = stem_ref[0], stem_ref[1]
    keep = [lane > 0, None, lane < 127]
    wz = [w0 if k is None else jnp.where(k, w0, 0.0) for k in keep]
    bz = [b0 if k is None else jnp.where(k, b0, 0.0) for k in keep]

    def norm(e, _):
        at = pl.multiple_of(e * 32, 32)
        v = est_ref[pl.ds(at, 32), :]
        v = (v.reshape(4, 8, 128) * scale[None]).reshape(32, 128)
        n_ref[1, pl.ds(at, 32), :] = v
        n_ref[0, pl.ds(at, 32), :] = pltpu.roll(v, 1, 1)
        n_ref[2, pl.ds(at, 32), :] = pltpu.roll(v, 127, 1)
        return 0

    lax.fori_loop(0, planes, norm, 0)
    f_ref[0:48, :] = jnp.zeros((48, 256), jnp.bfloat16)
    f_ref[33 * 48:34 * 48, :] = jnp.zeros((48, 256), jnp.bfloat16)
    m = ch * yb

    def pair(j, _):
        for s in range(2):
            e = 2 * j + s
            flag = jnp.where(e == 0, flag_ref[0], jnp.where(e == planes - 1, flag_ref[1], 1.0))
            at = pl.multiple_of(e * 32, 32)
            for dz in range(3):
                w, b = wz[dz] * flag, bz[dz] * flag
                for y in range(32):
                    row = jnp.broadcast_to(n_ref[dz, pl.ds(at + y, 1), :], (ch, 128))
                    f = jnp.maximum(w * row + b, 0.0).astype(jnp.bfloat16)
                    f_ref[(y + 1) * 48 + dz * 16:(y + 1) * 48 + dz * 16 + 16, s * 128:(s + 1) * 128] = f
        for k in range(32 // yb):
            p = jnp.dot(w_ref[...], f_ref[k * yb * 48:k * yb * 48 + (yb + 2) * 48, :], preferred_element_type=jnp.float32)
            pm, p0, pp = p[:m], p[m:2 * m], p[2 * m:]
            old = c_ref[k]
            done0 = old[:, :128] + pp[:, :128]
            done1 = old[:, 128:] + p0[:, :128] + pp[:, 128:]
            c_ref[k, :, :128] = pm[:, :128] + p0[:, 128:]
            c_ref[k, :, 128:] = pm[:, 128:]

            @pl.when(j > 0)
            def _():
                for s, d in enumerate((done0, done1)):
                    acc = None
                    for c in range(ch):
                        h = jnp.maximum(d[c * yb:(c + 1) * yb] + head_ref[0, c], 0.0) * head_ref[1, c]
                        acc = h if acc is None else acc + h
                    out_ref[pl.ds(pl.multiple_of((2 * j - 2 + s) * 32 + k * yb, 8), yb), :] = acc
        return 0

    c_ref[...] = jnp.zeros_like(c_ref)
    lax.fori_loop(0, planes // 2, pair, 0)


def conv_call(totals, flags, head, est, stem, w, count, yb=YB):
    planes = est.shape[0] // 32
    ch = head.shape[1]
    smem = pl.BlockSpec(memory_space=pltpu.SMEM)
    vmem = pl.BlockSpec(memory_space=pltpu.VMEM)
    return pl.pallas_call(
        functools.partial(conv_kernel, yb, count),
        out_shape=jax.ShapeDtypeStruct(((planes - 2) * 32, 128), jnp.float32),
        in_specs=[smem, smem, smem, vmem, vmem, vmem],
        out_specs=vmem,
        scratch_shapes=[
            pltpu.VMEM((3, planes * 32, 128), jnp.float32),
            pltpu.VMEM((34 * 48, 256), jnp.bfloat16),
            pltpu.VMEM((32 // yb, ch * yb, 256), jnp.float32),
        ],
        compiler_params=pltpu.CompilerParams(vmem_limit_bytes=48 * 2**20),
        cost_estimate=pl.CostEstimate(flops=4 * 10**9, bytes_accessed=2 * 10**6, transcendentals=0),
        name="conv_head",
    )(totals, flags, head, est, stem, w)


def shifted(cells, step):
    count = lax.axis_size("brick")
    pairs = [(i, i + step) for i in range(count) if 0 <= i + step < count]
    return lax.ppermute(cells, "brick", pairs)


def local(measured, psf, stem_params, conv_weight, head_params):
    views, plane_count, row_count, lane_count = measured.shape
    bricks = lax.axis_size("brick")
    early = jnp.mean(measured[:, :HALO].astype(F32), axis=0, keepdims=True).astype(BF16)
    late = jnp.mean(measured[:, HALO:].astype(F32), axis=0, keepdims=True).astype(BF16)
    lo = shifted(jnp.concatenate([measured[:, HALO:], early]), 1)
    hi = shifted(jnp.concatenate([measured[:, :HALO], late]), -1)
    kernels = psf / jnp.sum(psf, axis=-1, keepdims=True)
    *mats, bxt, bxt2, meast, est = prep_call(kernels, measured)
    est, estb, measx = first_call(lo, hi, meast, est, mats + [bxt])
    lo, hi = shifted(estb, 1), shifted(estb, -1)
    out, ext, mine = second_call(lo, hi, measx, est, mats + [bxt2], bricks)
    totals = lax.all_to_all(mine, "brick", 0, 0, tiled=True)
    place = lax.axis_index("brick")
    flags = jnp.stack([place > 0, place < bricks - 1]).astype(F32)
    stem = jnp.broadcast_to(stem_params[:, :, None], stem_params.shape + (lane_count,))
    cell_count = bricks * plane_count * row_count * lane_count
    logits = conv_call(totals, flags, head_params, ext, stem, conv_matrix(conv_weight), float(cell_count))
    shape = (plane_count, row_count, lane_count)
    return out.reshape(shape), logits.reshape(shape)


def solution(mesh):
    placed = (P(None, ("span", "brick"), None, None), P(), P(), P(), P())
    return jax.shard_map(
        local,
        mesh=mesh,
        in_specs=placed,
        out_specs=(P(("span", "brick"), None, None), P(("span", "brick"), None, None)),
        check_vma=False,
    )
```

profile of v0, /device:TPU:0, one launch (start us, length us, event | category | flops | bytes accessed | tf_op | source)
XLA Modules:
  0.0 127.3 jit_solution(12692097621617699983)
XLA Ops:
  0.7 1.4 %fusion.2 = (bf16[4,16,32,128]{3,2,1,0:T(8,128)(2,1)S(1)}, bf16[4,16,32,128]{3,2,1,0:T(8,128)(2,1)S(1)}) fusion(bf16[4,32,32,128]{3,2,1,0:T(8,128)(2,1)} %param.5), kind=kLoop, calls=%fused_computation.18 | loop fusion | bytes 2097152 | tf_op jit(solution)/shard_map/slice | solution.py:366
  2.1 1.4 %convert_reduce_fusion = (f32[16,32,128]{2,1,0:T(8,128)S(1)}, f32[16,32,128]{2,1,0:T(8,128)S(1)}) fusion(bf16[4,32,32,128]{3,2,1,0:T(8,128)(2,1)} %param.5), kind=kLoop, calls=%fused_computation | loop fusion | flops 917504 | bytes 1572864 | tf_op jit(solution)/shard_map/reduce_sum | solution.py:367
  3.5 0.9 pad_maximum_fusion
  4.4 2.4 %collective-permute-start = (bf16[5,16,32,128]{3,2,1,0:T(8,128)(2,1)}, bf16[5,16,32,128]{3,2,1,0:T(8,128)(2,1)S(1)}, u32[]{:S(2)}, u32[]{:S(2)}) collective-permute-start(bf16[5,16,32,128]{3,2,1,0:T(8,128)(2,1)} %pad_maximum_fusion), channel_id=1, source_target_pairs={{0,1},{1,2},{2,3},{3,4},{4,5},{5,6},{6,7},{7,8},{8,9},{9,10},{10,1... | collective-permute-start | bytes 1966088 | tf_op jit(solution)/shard_map/ppermute | solution.py:360
  6.8 0.9 pad_maximum_fusion.1
  7.7 1.3 %collective-permute-start.1 = (bf16[5,16,32,128]{3,2,1,0:T(8,128)(2,1)}, bf16[5,16,32,128]{3,2,1,0:T(8,128)(2,1)S(1)}, u32[]{:S(2)}, u32[]{:S(2)}) collective-permute-start(bf16[5,16,32,128]{3,2,1,0:T(8,128)(2,1)} %pad_maximum_fusion.1), channel_id=1, source_target_pairs={{1,0},{2,1},{3,2},{4,3},{5,4},{6,5},{7,6},{8,7},{9,8},{10,9},{11,1... | collective-permute-start | bytes 1966088 | tf_op jit(solution)/shard_map/ppermute | solution.py:360
  9.5 1.0 bitcast_dynamic-update-slice_fusion.7
  10.4 7.5 %bands_and_turn.1 = (bf16[256,96]{1,0:T(8,128)(2,1)S(1)}, bf16[2,256,256]{2,1,0:T(8,128)(2,1)S(1)}, bf16[2,256,256]{2,1,0:T(8,128)(2,1)S(1)}, bf16[4,256,256]{2,...) custom-call(f32[4,3,31]{2,1,0:T(4,128)S(1)} %copy_divide_fusion.k_re, ...), custom_call_target="tpu_custom_call" | custom-call | flops 1000000000 | bytes 20000000 | tf_op jit(solution)/shard_map/bands_and_turn/pallas_call | solution.py:84
  18.7 0.8 copy-done.4
  23.0 1.9 %bitcast_dynamic-update-slice_fusion.6 = bf16[8,3,10,3,16,16]{4,3,2,1,5,0:T(4,128)(2,1)} fusion(bf16[8,3,10,3,16,16]{4,3,2,1,5,0:T(4,128)(2,1)} %bitcast_dynamic-update-slice_fusion.7, bf16[3,3,3,16,16]{3,2,1,0,4:T(4,128)(2,1)} %copy-done.17), kind=kLoop, calls=%fused_computation.10 | loop fusion | bytes 638976
  24.9 1.9 %bitcast_dynamic-update-slice_fusion.5 = bf16[8,3,10,3,16,16]{4,3,2,1,5,0:T(4,128)(2,1)} fusion(bf16[8,3,10,3,16,16]{4,3,2,1,5,0:T(4,128)(2,1)} %bitcast_dynamic-update-slice_fusion.6, bf16[3,3,3,16,16]{3,2,1,0,4:T(4,128)(2,1)} %copy-done.17), kind=kLoop, calls=%fused_computation.9 | loop fusion | bytes 638976
  26.7 1.9 %bitcast_dynamic-update-slice_fusion.4 = bf16[8,3,10,3,16,16]{4,3,2,1,5,0:T(4,128)(2,1)} fusion(bf16[8,3,10,3,16,16]{4,3,2,1,5,0:T(4,128)(2,1)} %bitcast_dynamic-update-slice_fusion.5, bf16[3,3,3,16,16]{3,2,1,0,4:T(4,128)(2,1)} %copy-done.17), kind=kLoop, calls=%fused_computation.8 | loop fusion | bytes 638976
  28.6 1.8 %bitcast_dynamic-update-slice_fusion.3 = bf16[8,3,10,3,16,16]{4,3,2,1,5,0:T(4,128)(2,1)} fusion(bf16[8,3,10,3,16,16]{4,3,2,1,5,0:T(4,128)(2,1)} %bitcast_dynamic-update-slice_fusion.4, bf16[3,3,3,16,16]{3,2,1,0,4:T(4,128)(2,1)} %copy-done.17), kind=kLoop, calls=%fused_computation.7 | loop fusion | bytes 638976
  30.4 1.9 %bitcast_dynamic-update-slice_fusion.2 = bf16[8,3,10,3,16,16]{4,3,2,1,5,0:T(4,128)(2,1)} fusion(bf16[8,3,10,3,16,16]{4,3,2,1,5,0:T(4,128)(2,1)} %bitcast_dynamic-update-slice_fusion.3, bf16[3,3,3,16,16]{3,2,1,0,4:T(4,128)(2,1)} %copy-done.17), kind=kLoop, calls=%fused_computation.6 | loop fusion | bytes 638976
  32.3 1.0 copy-done.3
  33.4 1.0 copy-done.5
  34.4 1.0 copy-done.7
  35.4 0.9 copy-done.9
  36.4 0.9 copy-done.11
  37.3 0.8 copy-done.15
  38.2 11.4 %first_iteration.1 = (f32[32,32,128]{2,1,0:T(8,128)S(1)}, bf16[32,32,128]{2,1,0:T(8,128)(2,1)S(1)}, bf16[4,32,64,128]{3,2,1,0:T(8,128)(2,1)}) custom-call(bf16[5,512,128]{2,1,0:T(8,128)(2,1)S(1)} %bitcast.33, bf16[5,512,128]{2,1,0:T(8,128)(2,1)S(1)} %bitcast.34, bf16[4,32,32,128]{3,2,1,0:T(8,128)(2,1)S(1)} %get-tuple-element.17.meast_ref, ...), custom_call_target="tpu_custom_call" | custom-call | flops 6000000000 | bytes 8000000 | tf_op jit(solution)/shard_map/first_iteration/pallas_call | solution.py:229
  49.6 5.1 %collective-permute-start.2 = (bf16[32,32,128]{2,1,0:T(8,128)(2,1)S(1)}, bf16[32,32,128]{2,1,0:T(8,128)(2,1)S(1)}, u32[]{:S(2)}, u32[]{:S(2)}) collective-permute-start(bf16[32,32,128]{2,1,0:T(8,128)(2,1)S(1)} %get-tuple-element.25), channel_id=1, source_target_pairs={{0,1},{1,2},{2,3},{3,4},{4,5},{5,6},{6,7},{7,8},{8,9},{9,10},{10,1... | collective-permute-start | bytes 786440 | tf_op jit(solution)/shard_map/ppermute | solution.py:360
  54.8 1.3 %collective-permute-start.3 = (bf16[32,32,128]{2,1,0:T(8,128)(2,1)S(1)}, bf16[32,32,128]{2,1,0:T(8,128)(2,1)S(1)}, u32[]{:S(2)}, u32[]{:S(2)}) collective-permute-start(bf16[32,32,128]{2,1,0:T(8,128)(2,1)S(1)} %get-tuple-element.25), channel_id=1, source_target_pairs={{1,0},{2,1},{3,2},{4,3},{5,4},{6,5},{7,6},{8,7},{9,8},{10,9},{11,1... | collective-permute-start | bytes 786440 | tf_op jit(solution)/shard_map/ppermute | solution.py:360
  56.1 0.9 bitcast_dynamic-update-slice_fusion.1
  57.1 0.9 bitcast_dynamic-update-slice_fusion
  58.0 1.4 %collective-permute-done.3.hi_ref = bf16[32,32,128]{2,1,0:T(8,128)(2,1)S(1)} collective-permute-done((bf16[32,32,128]{2,1,0:T(8,128)(2,1)S(1)}, bf16[32,32,128]{2,1,0:T(8,128)(2,1)S(1)}, u32[]{:S(2)}, u32[]{:S(2)}) %collective-permute-start.3) | collective-permute-done | bytes 262176 | tf_op jit(solution)/shard_map/ppermute | solution.py:360
  59.4 1.6 %copy-done.16 = bf16[4,32,64,128]{3,2,1,0:T(8,128)(2,1)S(1)} copy-done((bf16[4,32,64,128]{3,2,1,0:T(8,128)(2,1)S(1)}, bf16[4,32,64,128]{3,2,1,0:T(8,128)(2,1)}, u32[]{:S(2)}) %copy-start.16) | copy-done | bytes 2097176
  61.0 9.2 %second_iteration.1 = (f32[1024,128]{1,0:T(8,128)}, f32[1088,128]{1,0:T(8,128)S(1)}, f32[16]{0:T(128)S(1)}) custom-call(bf16[32,32,128]{2,1,0:T(8,128)(2,1)S(1)} %collective-permute-done.2.lo_ref, bf16[32,32,128]{2,1,0:T(8,128)(2,1)S(1)} %collective-permute-done.3.hi_ref, bf16[4,32,64,128]{3,2,1,0:T(8,128)(2,1)S(1)} %copy-done.16, ...), custom_call_target="tpu_custom_call" | custom-call | flops 6000000000 | bytes 8000000 | tf_op jit(solution)/shard_map/second_iteration/pallas_call | solution.py:246
  70.9 11.1 %all-to-all-start = ((f32[16,1,1]{2,1,0:T(1,128)}), f32[16,1,1]{2,1,0:T(1,128)S(1)}, u32[]{:S(2)}, u32[]{:S(2)}) async-start(f32[16,1,1]{2,1,0:T(1,128)} %copy.24), calls=%async_computation | async-start | bytes 16384 | tf_op jit(solution)/shard_map/all_to_all | solution.py:375
  82.0 6.1 %copy.25 = bf16[3,16,8,10,3,16]{5,4,3,2,1,0:T(4,128)(2,1)} copy(bf16[3,16,8,10,3,16]{5,4,3,0,1,2:T(4,128)(2,1)} %bitcast.35) | data formatting | bytes 737280 | tf_op jit(solution)/shard_map/transpose | solution.py:271
  88.1 6.0 %reshape.64.w_ref = bf16[384,480]{1,0:T(8,128)(2,1)S(1)} reshape(bf16[3,16,8,10,3,16]{5,4,3,2,1,0:T(4,128)(2,1)} %copy.25) | data formatting | bytes 737280 | tf_op jit(solution)/shard_map/reshape | solution.py:272
  94.4 32.9 %conv_head.1 = f32[1024,128]{1,0:T(8,128)} custom-call(f32[16]{0:T(128)S(1)} %reduce.tot_ref, f32[2]{0:T(128)S(1)} %add_convert_fusion.flag_ref, f32[2,16]{1,0:T(2,128)S(1)} %copy-done.1, f32[1088,128]{1,0:T(8,128)S(1)} %get-tuple-element.31.est_ref, f32[2,16,128]{2,1,0:T(8,128)S(1)} %broadcast_in_dim.2.stem_ref, bf16[384,480]{1,0:T(8,128)(2,1)S(1)} %reshape.64.w_ref), custom_call_target="tpu_custom_call" | custom-call | flops 4000000000 | bytes 2000000 | tf_op jit(solution)/shard_map/conv_head/pallas_call | solution.py:341
  (50 shorter events, 5.8 us)
Async XLA Ops:
  0.6 9.8 %copy-start = (bf16[4,32,32,128]{3,2,1,0:T(8,128)(2,1)S(1)}, bf16[4,32,32,128]{3,2,1,0:T(8,128)(2,1)}, u32[]{:S(2)}) copy-start(bf16[4,32,32,128]{3,2,1,0:T(8,128)(2,1)} %param.5) | copy-start | bytes 3145732
  0.6 8.4 %copy-start.19 = (f32[4,3,31]{2,0,1:T(4,128)S(1)}, f32[4,3,31]{2,0,1:T(4,128)}, u32[]{:S(2)}) copy-start(f32[4,3,31]{2,0,1:T(4,128)} %param.6) | copy-start | bytes 4468
  0.7 8.6 %copy-start.20 = (bf16[432,16]{0,1:T(8,128)(2,1)S(1)}, bf16[432,16]{0,1:T(8,128)(2,1)}, u32[]{:S(2)}) copy-start(bf16[432,16]{0,1:T(8,128)(2,1)} %param.8) | copy-start | bytes 41476
  4.4 27.9 %collective-permute-start = (bf16[5,16,32,128]{3,2,1,0:T(8,128)(2,1)}, bf16[5,16,32,128]{3,2,1,0:T(8,128)(2,1)S(1)}, u32[]{:S(2)}, u32[]{:S(2)}) collective-permute-start(bf16[5,16,32,128]{3,2,1,0:T(8,128)(2,1)} %pad_maximum_fusion), channel_id=1, source_target_pairs={{0,1},{1,2},{2,3},{3,4},{4,5},{5,6},{6,7},{7,8},{8,9},{9,10},{10,1... | collective-permute-start | bytes 1966088 | tf_op jit(solution)/shard_map/ppermute | solution.py:360
  7.7 24.6 %collective-permute-start.1 = (bf16[5,16,32,128]{3,2,1,0:T(8,128)(2,1)}, bf16[5,16,32,128]{3,2,1,0:T(8,128)(2,1)S(1)}, u32[]{:S(2)}, u32[]{:S(2)}) collective-permute-start(bf16[5,16,32,128]{3,2,1,0:T(8,128)(2,1)} %pad_maximum_fusion.1), channel_id=1, source_target_pairs={{1,0},{2,1},{3,2},{4,3},{5,4},{6,5},{7,6},{8,7},{9,8},{10,9},{11,1... | collective-permute-start | bytes 1966088 | tf_op jit(solution)/shard_map/ppermute | solution.py:360
  9.4 1.0 copy-start.17
  17.9 0.8 copy-start.2
  18.7 0.8 copy-start.4
  19.5 0.8 copy-start.6
  20.3 0.7 copy-start.8
  21.0 0.7 copy-start.10
  21.7 0.7 copy-start.12
  22.4 0.6 copy-start.14
  32.3 1.0 copy-start.3
  33.4 1.0 copy-start.5
  34.4 1.0 copy-start.7
  35.4 0.9 copy-start.9
  36.4 0.9 copy-start.11
  37.3 0.8 copy-start.15
  38.2 18.0 %copy-start.18 = (bf16[3,3,3,16,16]{3,2,1,0,4:T(4,128)(2,1)S(1)}, bf16[3,3,3,16,16]{3,2,1,0,4:T(4,128)(2,1)}, u32[]{:S(2)}) copy-start(bf16[3,3,3,16,16]{3,2,1,0,4:T(4,128)(2,1)} %copy-done.17) | copy-start | bytes 41476
  38.2 21.2 %copy-start.13 = (bf16[192,512]{1,0:T(8,128)(2,1)S(1)}, bf16[192,512]{1,0:T(8,128)(2,1)}, u32[]{:S(2)}) copy-start(bf16[192,512]{1,0:T(8,128)(2,1)} %copy-done.12) | copy-start | bytes 589828
  49.6 8.4 %collective-permute-start.2 = (bf16[32,32,128]{2,1,0:T(8,128)(2,1)S(1)}, bf16[32,32,128]{2,1,0:T(8,128)(2,1)S(1)}, u32[]{:S(2)}, u32[]{:S(2)}) collective-permute-start(bf16[32,32,128]{2,1,0:T(8,128)(2,1)S(1)} %get-tuple-element.25), channel_id=1, source_target_pairs={{0,1},{1,2},{2,3},{3,4},{4,5},{5,6},{6,7},{7,8},{8,9},{9,10},{10,1... | collective-permute-start | bytes 786440 | tf_op jit(solution)/shard_map/ppermute | solution.py:360
  54.8 4.7 %collective-permute-start.3 = (bf16[32,32,128]{2,1,0:T(8,128)(2,1)S(1)}, bf16[32,32,128]{2,1,0:T(8,128)(2,1)S(1)}, u32[]{:S(2)}, u32[]{:S(2)}) collective-permute-start(bf16[32,32,128]{2,1,0:T(8,128)(2,1)S(1)} %get-tuple-element.25), channel_id=1, source_target_pairs={{1,0},{2,1},{3,2},{4,3},{5,4},{6,5},{7,6},{8,7},{9,8},{10,9},{11,1... | collective-permute-start | bytes 786440 | tf_op jit(solution)/shard_map/ppermute | solution.py:360
  59.4 1.6 %copy-start.16 = (bf16[4,32,64,128]{3,2,1,0:T(8,128)(2,1)S(1)}, bf16[4,32,64,128]{3,2,1,0:T(8,128)(2,1)}, u32[]{:S(2)}) copy-start(bf16[4,32,64,128]{3,2,1,0:T(8,128)(2,1)} %get-tuple-element.26.measx_ref) | copy-start | bytes 6291460
  70.9 23.2 %all-to-all-start = ((f32[16,1,1]{2,1,0:T(1,128)}), f32[16,1,1]{2,1,0:T(1,128)S(1)}, u32[]{:S(2)}, u32[]{:S(2)}) async-start(f32[16,1,1]{2,1,0:T(1,128)} %copy.24), calls=%async_computation | async-start | bytes 16384 | tf_op jit(solution)/shard_map/all_to_all | solution.py:375
  88.1 6.2 %copy-start.21 = (f32[2,16]{1,0:T(2,128)S(1)}, f32[2,16]{1,0:T(2,128)}, u32[]{:S(2)}) copy-start(f32[2,16]{1,0:T(2,128)} %param.7) | copy-start | bytes 388
  88.1 6.3 %copy-start.1 = (f32[2,16]{1,0:T(2,128)S(1)}, f32[2,16]{1,0:T(2,128)}, u32[]{:S(2)}) copy-start(f32[2,16]{1,0:T(2,128)} %head_ref.1) | copy-start | bytes 388
where the time goes:
time: 128 us; the launch traced here: 127 us
  Pallas kernels  61 us (48%)
  local copies, waits for them, and re-layouts  39.2 us (31%)
  starting transfers between devices  21.2 us (17%)
  other arithmetic  3.7 us (3%)
  waiting for transfers between devices  1.4 us (1%)
    pallas_call x1, Pallas kernels, conv_call(): pl.pallas_call(functools.partial(conv_kernel, yb, count), out_shape=jax.S...  32.9 us
    unnamed x51, local copies, waits for them, and re-layouts  23.8 us
    pallas_call x1, Pallas kernels, first_call(): pl.pallas_call(first_kernel, out_shape=[jax.ShapeDtypeStruct((32, 32, 128...  11.4 us
    all_to_all x1, starting transfers between devices, local(): totals = lax.all_to_all(mine, 'brick', 0, 0, tiled=True)  11.1 us
    ppermute x4, starting transfers between devices, shifted(): return lax.ppermute(cells, 'brick', pairs)  10.1 us
    pallas_call x1, Pallas kernels, second_call(): pl.pallas_call(second_kernel, out_shape=[jax.ShapeDtypeStruct((1024, 128)...  9.18 us
    pallas_call x1, Pallas kernels, prep_call(): pl.pallas_call(prep_kernel, out_shape=[jax.ShapeDtypeStruct(s, d) for s,...  7.49 us
    transpose x1, local copies, waits for them, and re-layouts, conv_matrix(): m = m.transpose(1, 5, 0, 2, 3, 4)  6.13 us
  transfers between devices with their start and end apart: 5, of which 1 were waited for; matrix products, arithmetic and copies ran while one was open for 20% of the time, Pallas kernels for 6%

commit v1 on v0

v1 whole, which is shorter than its diff:
```python
import functools
import jax, jax.numpy as jnp
from jax import lax
from jax.experimental import pallas as pl
from jax.experimental.pallas import tpu as pltpu
from jax.sharding import PartitionSpec as P

F32, BF16 = jnp.float32, jnp.bfloat16
HALO = 16
SMEM = pl.BlockSpec(memory_space=pltpu.SMEM)
VMEM = pl.BlockSpec(memory_space=pltpu.VMEM)


def iotas(shape):
    return lax.broadcasted_iota(jnp.int32, shape, 0), lax.broadcasted_iota(jnp.int32, shape, 1)


def bands(k_ref, dim, index):
    views, taps = k_ref.shape[0], k_ref.shape[2]
    out = [jnp.zeros(index.shape, F32)] * views
    for t in range(taps):
        hit = index == t
        out = [jnp.where(hit, k_ref[v, dim, t], out[v]) for v in range(views)]
    return out


def prep_kernel(k_ref, meas_ref, kx_ref, bz_ref, bzt_ref, ly_ref, lyt_ref, bxt_ref, bxt2_ref, meast_ref, est_ref, nat_ref):
    views = k_ref.shape[0]
    reach = (k_ref.shape[2] - 1) // 2
    r, c = iotas((64, 96))
    for v, m in enumerate(bands(k_ref, 0, c - r - HALO + reach)):
        kx_ref[v * 64:(v + 1) * 64, :] = m.astype(BF16)
    for ref, rows, first in ((bxt_ref, 32, 0), (bxt2_ref, 48, -8)):
        r, c = iotas((rows, 512))
        for v, m in enumerate(bands(k_ref, 0, (r + first) - ((c & 63) - HALO) + reach)):
            ref[v * rows:(v + 1) * rows, :] = jnp.where(((c >> 6) & 3) == v, m, 0.0).astype(BF16)
    r, c = iotas((128, 128))
    zero = jnp.zeros((128, 128), BF16)
    for ref, sign in ((bz_ref, 1), (bzt_ref, -1)):
        for v, m in enumerate(bands(k_ref, 2, sign * (r - c) + reach)):
            p, a = v // 2, v % 2
            ref[p, a * 128:(a + 1) * 128, a * 128:(a + 1) * 128] = m.astype(BF16)
            ref[p, a * 128:(a + 1) * 128, (1 - a) * 128:(2 - a) * 128] = zero
    r, c = iotas((32, 32))
    er, ec = iotas((256, 32))
    spread = ((er >> 3) == ec).astype(F32).astype(BF16)
    tr, tc = iotas((32, 256))
    spread_t = ((tc >> 3) == tr).astype(F32).astype(BF16)
    fr, fc = iotas((256, 256))
    same = (fr & 7) == (fc & 7)
    for ref, sign in ((ly_ref, 1), (lyt_ref, -1)):
        for v, m in enumerate(bands(k_ref, 1, sign * (c - r) + reach)):
            wide = jnp.dot(spread, m.astype(BF16), preferred_element_type=F32).astype(BF16)
            full = jnp.dot(wide, spread_t, preferred_element_type=F32)
            ref[v] = jnp.where(same, full, 0.0).astype(BF16)
    for v in range(views):
        nat_ref[v] = meas_ref[v].astype(F32)

    def turn(y, _):
        acc = None
        for v in range(views):
            m = nat_ref[v, pl.ds(y, 32, stride=32), :]
            acc = m if acc is None else acc + m
            meast_ref[v, y] = m.astype(BF16)
        est_ref[y] = acc * (1.0 / views)
        return 0

    lax.fori_loop(0, 32, turn, 0)


def prep_call(kernels, measured):
    views = measured.shape[0]
    out = [
        ((views * 64, 96), BF16),
        ((2, 256, 256), BF16),
        ((2, 256, 256), BF16),
        ((views, 256, 256), BF16),
        ((views, 256, 256), BF16),
        ((views * 32, 512), BF16),
        ((views * 48, 512), BF16),
        ((views, 32, 32, 128), BF16),
        ((32, 32, 128), F32),
    ]
    return pl.pallas_call(
        prep_kernel,
        out_shape=[jax.ShapeDtypeStruct(s, d) for s, d in out],
        in_specs=[SMEM, VMEM],
        out_specs=[VMEM] * len(out),
        scratch_shapes=[pltpu.VMEM((views, 1024, 128), F32)],
        compiler_params=pltpu.CompilerParams(vmem_limit_bytes=16 * 2**20),
        cost_estimate=pl.CostEstimate(flops=10**9, bytes_accessed=20 * 10**6, transcendentals=0),
        name="bands_and_turn",
    )(kernels, measured.reshape(views, 1024, 128))


XN, ZM, YN, XT = 8, 8, 8, 8


def correct(eb_ref, meas, kx_ref, bz_ref, bzt_ref, ly_ref, lyt_ref, bxt_ref, rows, a_ref, b_ref, c_ref, d_ref, finish):
    for k in range(32 // XN):
        at = k * XN * 128
        p = jnp.dot(kx_ref[...], eb_ref[:, at:at + XN * 128], preferred_element_type=F32)
        a_ref[:, at:at + XN * 128] = p.astype(BF16)

    for k in range(32 // ZM):
        for p in range(2):
            tall = []
            for y in range(k * ZM, k * ZM + ZM):
                tall.append(jnp.concatenate([a_ref[(2 * p + a) * 64:(2 * p + a) * 64 + 64, y * 128:y * 128 + 128] for a in range(2)], axis=1))
            q = jnp.dot(jnp.concatenate(tall, axis=0), bz_ref[p], preferred_element_type=F32)
            for a in range(2):
                b_ref[2 * p + a, k * ZM:k * ZM + ZM] = q[:, a * 128:(a + 1) * 128].reshape(ZM, 64, 128)

    for v in range(4):
        for k in range(8 // YN):
            x0 = k * YN * 8
            wide = [b_ref[v, :, x0 + 8 * a:x0 + 8 * a + 8, :].reshape(256, 128).astype(BF16) for a in range(YN)]
            q = jnp.dot(ly_ref[v], jnp.concatenate(wide, axis=1), preferred_element_type=F32)
            wide = []
            for h in range(YN // 2):
                m = meas[v, :, x0 + 16 * h:x0 + 16 * h + 16, :].astype(F32)
                for a in range(2):
                    top = m[:, 8 * a:8 * a + 8, :].reshape(256, 128)
                    at = (2 * h + a) * 128
                    ratio = jnp.where(top > 0.0, top / q[:, at:at + 128], 0.0)
                    wide.append(ratio.astype(BF16))
            q = jnp.dot(lyt_ref[v], jnp.concatenate(wide, axis=1), preferred_element_type=F32)
            for h in range(YN // 2):
                pair = [q[:, (2 * h + a) * 128:(2 * h + a + 1) * 128].reshape(32, 8, 128) for a in range(2)]
                c_ref[v, :, x0 + 16 * h:x0 + 16 * h + 16, :] = jnp.concatenate(pair, axis=1).astype(BF16)

    for k in range(32 // ZM):
        for p in range(2):
            tall = jnp.concatenate([c_ref[2 * p + a, k * ZM:k * ZM + ZM].reshape(ZM * 64, 128) for a in range(2)], axis=1)
            q = jnp.dot(tall, bzt_ref[p], preferred_element_type=F32)
            for a in range(2):
                at = (2 * p + a) * 64
                for y in range(ZM):
                    w = q[y * 64:y * 64 + 64, a * 128:(a + 1) * 128]
                    hi = w.astype(BF16)
                    col = (k * ZM + y) * 128
                    d_ref[at:at + 64, col:col + 128] = hi
                    d_ref[256 + at:256 + at + 64, col:col + 128] = (w - hi.astype(F32)).astype(BF16)

    carry = jnp.zeros((8, 128), F32)
    for k in range(32 // XT):
        p = jnp.dot(bxt_ref[...], d_ref[:, k * XT * 128:(k + 1) * XT * 128], preferred_element_type=F32)
        for y in range(XT):
            f = None
            for v in range(4):
                g = p[v * rows:(v + 1) * rows, y * 128:(y + 1) * 128]
                f = g if f is None else f * g
            carry = finish(k * XT + y, f, carry)
    return carry


def first_kernel(lo_ref, hi_ref, meast_ref, est_ref, kx, bz, bzt, ly, lyt, bxt, new_ref, newb_ref, measx_ref,
                 nat_ref, eb_ref, a_ref, b_ref, c_ref, d_ref):
    for side, ref in enumerate((lo_ref, hi_ref)):
        for v in range(5):
            nat_ref[side, v] = ref[v].astype(F32)

    def turn(y, _):
        col = pl.multiple_of(y * 128, 128)
        for side, near, far, at in ((0, 16, 0, 0), (1, 64, 80, 48)):
            acc = None
            for v in range(4):
                m = nat_ref[side, v, pl.ds(y, 16, stride=32), :]
                acc = m if acc is None else acc + m
                measx_ref[v, y, at:at + 16, :] = m.astype(BF16)
            eb_ref[near:near + 16, pl.ds(col, 128)] = (acc * 0.25).astype(BF16)
            eb_ref[far:far + 16, pl.ds(col, 128)] = nat_ref[side, 4, pl.ds(y, 16, stride=32), :].astype(BF16)
        for v in range(4):
            measx_ref[v, y, 16:48, :] = meast_ref[v, y]
        eb_ref[32:64, pl.ds(col, 128)] = est_ref[y].astype(BF16)
        return 0

    lax.fori_loop(0, 32, turn, 0, unroll=2)

    def finish(y, f, carry):
        e = est_ref[y] * f
        new_ref[y] = e
        newb_ref[y] = e.astype(BF16)
        return carry

    correct(eb_ref, measx_ref, kx, bz, bzt, ly, lyt, bxt, 32, a_ref, b_ref, c_ref, d_ref, finish)


def second_kernel(lo_ref, hi_ref, measx_ref, est_ref, kx, bz, bzt, ly, lyt, bxt, out_ref, ext_ref, sum_ref,
                  eb_ref, a_ref, b_ref, c_ref, d_ref):
    def fill(y, _):
        col = pl.multiple_of(y * 128, 128)
        eb_ref[0:32, pl.ds(col, 128)] = lo_ref[y]
        eb_ref[32:64, pl.ds(col, 128)] = est_ref[y].astype(BF16)
        eb_ref[64:96, pl.ds(col, 128)] = hi_ref[y]
        return 0

    lax.fori_loop(0, 32, fill, 0, unroll=2)

    def finish(y, f, carry):
        mid = est_ref[y] * f[8:40]
        before = lo_ref[y, 16:32, :].astype(F32)[8:16] * f[0:8]
        after = hi_ref[y, 0:16, :].astype(F32)[0:8] * f[40:48]
        out_ref[pl.ds(y, 32, stride=32), :] = mid
        ext_ref[pl.ds(32 + y, 32, stride=32), :] = mid
        ext_ref[pl.ds(y, 1), :] = before[7:8]
        ext_ref[pl.ds(33 * 32 + y, 1), :] = after[0:1]
        return carry + ((mid[0:8] + mid[8:16]) + (mid[16:24] + mid[24:32]))

    total = correct(eb_ref, measx_ref, kx, bz, bzt, ly, lyt, bxt, 48, a_ref, b_ref, c_ref, d_ref, finish)
    whole = jnp.sum(total)
    for k in range(sum_ref.shape[0]):
        sum_ref[k] = whole


SCRATCH = [
    pltpu.VMEM((96, 4096), BF16),
    pltpu.VMEM((256, 4096), BF16),
    pltpu.VMEM((4, 32, 64, 128), F32),
    pltpu.VMEM((4, 32, 64, 128), BF16),
    pltpu.VMEM((512, 4096), BF16),
]
COST = pl.CostEstimate(flops=6 * 10**9, bytes_accessed=8 * 10**6, transcendentals=0)


def first_call(lo, hi, meast, est, mats):
    return pl.pallas_call(
        first_kernel,
        out_shape=[
            jax.ShapeDtypeStruct((32, 32, 128), F32),
            jax.ShapeDtypeStruct((32, 32, 128), BF16),
            jax.ShapeDtypeStruct((4, 32, 64, 128), BF16),
        ],
        in_specs=[VMEM] * 10,
        out_specs=[VMEM] * 3,
        scratch_shapes=[pltpu.VMEM((2, 5, 512, 128), F32)] + SCRATCH,
        compiler_params=pltpu.CompilerParams(vmem_limit_bytes=32 * 2**20),
        cost_estimate=COST,
        name="first_iteration",
    )(lo.reshape(5, 512, 128), hi.reshape(5, 512, 128), meast, est, *mats)


def second_call(lo, hi, measx, est, mats, bricks):
    return pl.pallas_call(
        second_kernel,
        out_shape=[
            jax.ShapeDtypeStruct((1024, 128), F32),
            jax.ShapeDtypeStruct((34 * 32, 128), F32),
            jax.ShapeDtypeStruct((bricks,), F32),
        ],
        in_specs=[VMEM] * 10,
        out_specs=[VMEM, VMEM, SMEM],
        scratch_shapes=SCRATCH,
        compiler_params=pltpu.CompilerParams(vmem_limit_bytes=32 * 2**20),
        cost_estimate=COST,
        name="second_iteration",
    )(lo, hi, measx, est, *mats)

YB = 3


def conv_matrix(conv_weight, yb=YB):
    ch = conv_weight.shape[1]
    w = conv_weight.T.reshape(ch, 3, 9 * ch)
    step = 3 * ch
    rows = [jnp.pad(w, ((0, 0), (0, 0), (yo * step, (yb - 1 - yo) * step))) for yo in range(yb)]
    m = jnp.stack(rows, 0)
    return m.transpose(2, 0, 1, 3).reshape(3 * yb * ch, (yb + 2) * step)


def fold_channels(parts):
    sub = lax.broadcasted_iota(jnp.int32, (8, 128), 0)
    for width in (4, 2, 1):
        keep = (sub & width) == 0
        half = len(parts) // 2
        merged = []
        for k in range(half):
            a, b = parts[k], parts[k + half]
            swap = jnp.where(keep, b, a)
            merged.append(jnp.where(keep, a, b) + pltpu.roll(swap, width, 0) if width == 4 else
                          jnp.where(keep, a + pltpu.roll(a, 8 - width, 0), b + pltpu.roll(b, width, 0)))
        parts = merged
    return parts[0]


def conv_kernel(count, tot_ref, flag_ref, est_ref, stem_ref, head_ref, w_ref, out_ref, n_ref, f_ref, p_ref):
    planes = est_ref.shape[0] // 32
    ch = stem_ref.shape[1]
    total = tot_ref[0]
    for k in range(1, tot_ref.shape[0]):
        total = total + tot_ref[k]
    scale = count / jnp.full((8, 128), total, jnp.float32)
    lane = lax.broadcasted_iota(jnp.int32, (ch, 128), 1)
    w0, b0 = stem_ref[0], stem_ref[1]
    keep = [lane > 0, None, lane < 127]
    wz = [w0 if k is None else jnp.where(k, w0, 0.0) for k in keep]
    bz = [b0 if k is None else jnp.where(k, b0, 0.0) for k in keep]

    blank = jnp.zeros((48, planes * 128), jnp.bfloat16)
    for y in (0, 33, 34):
        f_ref[y * 48:(y + 1) * 48, :] = blank

    def plane(e, _):
        at = pl.multiple_of(e * 32, 32)
        col = pl.multiple_of(e * 128, 128)
        v = est_ref[pl.ds(at, 32), :]
        v = (v.reshape(4, 8, 128) * scale[None]).reshape(32, 128)
        n_ref[0] = pltpu.roll(v, 1, 1)
        n_ref[1] = v
        n_ref[2] = pltpu.roll(v, 127, 1)
        flag = jnp.where(e == 0, flag_ref[0], jnp.where(e == planes - 1, flag_ref[1], 1.0))
        for dz in range(3):
            w, b = wz[dz] * flag, bz[dz] * flag
            for y in range(32):
                row = jnp.broadcast_to(n_ref[dz, y:y + 1, :], (ch, 128))
                f = jnp.maximum(w * row + b, 0.0).astype(jnp.bfloat16)
                f_ref[(y + 1) * 48 + dz * 16:(y + 1) * 48 + dz * 16 + 16, pl.ds(col, 128)] = f
        return 0

    lax.fori_loop(0, planes, plane, 0)
    bias = [head_ref[0, 0:8], head_ref[0, 8:16]]
    gain = [head_ref[1, 0:8], head_ref[1, 8:16]]
    m = YB * ch

    def block(k, _):
        at = pl.multiple_of(k * (YB * 48), 16)
        p_ref[...] = jnp.dot(w_ref[...], f_ref[pl.ds(at, (YB + 2) * 48), :], preferred_element_type=jnp.float32)
        for yo in range(YB):
            rows = []
            for g in range((planes - 2) // 8):
                parts = []
                for o in range(g * 8, g * 8 + 8):
                    s = None
                    for h in range(2):
                        top = yo * ch + h * 8
                        acc = (p_ref[top:top + 8, o * 128:o * 128 + 128]
                               + p_ref[m + top:m + top + 8, o * 128 + 128:o * 128 + 256]
                               + p_ref[2 * m + top:2 * m + top + 8, o * 128 + 256:o * 128 + 384])
                        acc = jnp.maximum(acc + bias[h], 0.0) * gain[h]
                        s = acc if s is None else s + acc
                    parts.append(s)
                rows.append(fold_channels(parts))

            def put():
                for g, r in enumerate(rows):
                    out_ref[pl.ds(g * 256 + k * YB + yo, 8, stride=32), :] = r

            if yo == YB - 1:
                pl.when(k * YB + yo < 32)(put)
            else:
                put()
        return 0

    lax.fori_loop(0, 11, block, 0)


def conv_call(totals, flags, head, est, stem, w, count):
    planes = est.shape[0] // 32
    ch = head.shape[1]
    smem = pl.BlockSpec(memory_space=pltpu.SMEM)
    vmem = pl.BlockSpec(memory_space=pltpu.VMEM)
    return pl.pallas_call(
        functools.partial(conv_kernel, count),
        out_shape=jax.ShapeDtypeStruct(((planes - 2) * 32, 128), jnp.float32),
        in_specs=[smem, smem, vmem, vmem, vmem, vmem],
        out_specs=vmem,
        scratch_shapes=[
            pltpu.VMEM((3, 32, 128), jnp.float32),
            pltpu.VMEM((35 * 48, planes * 128), jnp.bfloat16),
            pltpu.VMEM((3 * YB * ch, planes * 128), jnp.float32),
        ],
        compiler_params=pltpu.CompilerParams(vmem_limit_bytes=40 * 2**20),
        cost_estimate=pl.CostEstimate(flops=4 * 10**9, bytes_accessed=2 * 10**6, transcendentals=0),
        name="conv_head",
    )(totals, flags, est, stem, jnp.broadcast_to(head[:, :, None], (2, ch, 128)), w)


def shifted(cells, step):
    count = lax.axis_size("brick")
    pairs = [(i, i + step) for i in range(count) if 0 <= i + step < count]
    return lax.ppermute(cells, "brick", pairs)


def local(measured, psf, stem_params, conv_weight, head_params):
    views, plane_count, row_count, lane_count = measured.shape
    bricks = lax.axis_size("brick")
    early = jnp.mean(measured[:, :HALO].astype(F32), axis=0, keepdims=True).astype(BF16)
    late = jnp.mean(measured[:, HALO:].astype(F32), axis=0, keepdims=True).astype(BF16)
    lo = shifted(jnp.concatenate([measured[:, HALO:], early]), 1)
    hi = shifted(jnp.concatenate([measured[:, :HALO], late]), -1)
    kernels = psf / jnp.sum(psf, axis=-1, keepdims=True)
    *mats, bxt, bxt2, meast, est = prep_call(kernels, measured)
    est, estb, measx = first_call(lo, hi, meast, est, mats + [bxt])
    lo, hi = shifted(estb, 1), shifted(estb, -1)
    out, ext, mine = second_call(lo, hi, measx, est, mats + [bxt2], bricks)
    totals = lax.all_to_all(mine, "brick", 0, 0, tiled=True)
    place = lax.axis_index("brick")
    flags = jnp.stack([place > 0, place < bricks - 1]).astype(F32)
    stem = jnp.broadcast_to(stem_params[:, :, None], stem_params.shape + (lane_count,))
    cell_count = bricks * plane_count * row_count * lane_count
    logits = conv_call(totals, flags, head_params, ext, stem, conv_matrix(conv_weight), float(cell_count))
    shape = (plane_count, row_count, lane_count)
    return out.reshape(shape), logits.reshape(shape)


def solution(mesh):
    placed = (P(None, ("span", "brick"), None, None), P(), P(), P(), P())
    return jax.shard_map(
        local,
        mesh=mesh,
        in_specs=placed,
        out_specs=(P(("span", "brick"), None, None), P(("span", "brick"), None, None)),
        check_vma=False,
    )
```

time: 128 us -> 79.5 us (0.62)
  local copies, waits for them, and re-layouts: 39.2 us -> 10.3 us
  Pallas kernels: 61 us -> 32.8 us
  waiting for transfers between devices: 1.4 us -> 9.74 us
  starting transfers between devices: 21.2 us -> 22.8 us
    pallas_call x1, Pallas kernels: 32.9 us -> 12.3 us  [conv_call(): pl.pallas_call(functools.partial(conv_kernel, count), out_shape=jax.Shape...]
    unnamed x51 -> x30, local copies, waits for them, and re-layouts: 23.8 us -> 7.74 us
    all_to_all x1, waiting for transfers between devices: 0.01 us -> 6.24 us  [local(): totals = lax.all_to_all(mine, 'brick', 0, 0, tiled=True)]
    transpose x1, local copies, waits for them, and re-layouts: 6.13 us -> 0.01 us  [conv_matrix(): return m.transpose(2, 0, 1, 3).reshape(3 * yb * ch, (yb + 2) * step)]
    reshape x2 -> x1, local copies, waits for them, and re-layouts: 6.14 us -> 0.09 us  [conv_matrix(): w = conv_weight.T.reshape(ch, 3, 9 * ch)]
    ppermute x4, starting transfers between devices: 10.1 us -> 14.4 us  [shifted(): return lax.ppermute(cells, 'brick', pairs)]
    pallas_call x1, Pallas kernels: 11.4 us -> 7.18 us  [first_call(): pl.pallas_call(first_kernel, out_shape=[jax.ShapeDtypeStruct((32, 32, 128...]
    pallas_call x1, Pallas kernels: 9.18 us -> 5.91 us  [second_call(): pl.pallas_call(second_kernel, out_shape=[jax.ShapeDtypeStruct((1024, 128)...]
  transfers between devices with their start and end apart: 5 -> 5, of which waited for: 1 -> 2; matrix products, arithmetic and copies ran while one was open for 20% -> 2% of each run, Pallas kernels for 6% -> 9%
where the time goes in v1:
time: 79.5 us; the launch traced here: 79.1 us
  Pallas kernels  32.8 us (41%)
  starting transfers between devices  22.8 us (29%)
  local copies, waits for them, and re-layouts  10.3 us (13%)
  waiting for transfers between devices  9.74 us (12%)
  other arithmetic  2.58 us (3%)
  between operations  0.88 us (1%)
    ppermute x4, starting transfers between devices, shifted(): return lax.ppermute(cells, 'brick', pairs)  14.4 us
    pallas_call x1, Pallas kernels, conv_call(): pl.pallas_call(functools.partial(conv_kernel, count), out_shape=jax.Shape...  12.3 us
    all_to_all x1, starting transfers between devices, local(): totals = lax.all_to_all(mine, 'brick', 0, 0, tiled=True)  8.44 us
    unnamed x30, local copies, waits for them, and re-layouts  7.74 us
    pallas_call x1, Pallas kernels, prep_call(): pl.pallas_call(prep_kernel, out_shape=[jax.ShapeDtypeStruct(s, d) for s,...  7.49 us
    pallas_call x1, Pallas kernels, first_call(): pl.pallas_call(first_kernel, out_shape=[jax.ShapeDtypeStruct((32, 32, 128...  7.18 us
    all_to_all x1, waiting for transfers between devices, local(): totals = lax.all_to_all(mine, 'brick', 0, 0, tiled=True)  6.24 us
    pallas_call x1, Pallas kernels, second_call(): pl.pallas_call(second_kernel, out_shape=[jax.ShapeDtypeStruct((1024, 128)...  5.91 us
  transfers between devices with their start and end apart: 5, of which 2 were waited for; matrix products, arithmetic and copies ran while one was open for 2% of the time, Pallas kernels for 9%

profile of v1, /device:TPU:0, one launch (start us, length us, event | category | flops | bytes accessed | tf_op | source)
XLA Modules:
  0.0 79.1 jit_solution(3670024587798151418)
XLA Ops:
  0.6 1.4 %fusion.2 = (bf16[4,16,32,128]{3,2,1,0:T(8,128)(2,1)S(1)}, bf16[4,16,32,128]{3,2,1,0:T(8,128)(2,1)S(1)}) fusion(bf16[4,32,32,128]{3,2,1,0:T(8,128)(2,1)} %param.5), kind=kLoop, calls=%fused_computation.14 | loop fusion | bytes 2097152 | tf_op jit(solution)/shard_map/slice | solution.py:387
  2.0 0.1 copy-done
  2.2 0.2 convert_reduce_fusion
  2.4 0.9 %pad_maximum_fusion = bf16[5,16,32,128]{3,2,1,0:T(8,128)(2,1)} fusion(bf16[1,16,32,128]{3,2,1,0:T(8,128)(2,1)S(1)} %fusion, bf16[4,16,32,128]{3,2,1,0:T(8,128)(2,1)S(1)} %get-tuple-element.35), kind=kLoop, calls=%fused_computation.2 | loop fusion | flops 327680 | bytes 1310720 | tf_op jit(solution)/shard_map/concatenate | solution.py:389
  3.3 2.4 %collective-permute-start = (bf16[5,16,32,128]{3,2,1,0:T(8,128)(2,1)}, bf16[5,16,32,128]{3,2,1,0:T(8,128)(2,1)S(1)}, u32[]{:S(2)}, u32[]{:S(2)}) collective-permute-start(bf16[5,16,32,128]{3,2,1,0:T(8,128)(2,1)} %pad_maximum_fusion), channel_id=1, source_target_pairs={{0,1},{1,2},{2,3},{3,4},{4,5},{5,6},{6,7},{7,8},{8,9},{9,10},{10,1... | collective-permute-start | bytes 1966088 | tf_op jit(solution)/shard_map/ppermute | solution.py:381
  5.7 0.9 %pad_maximum_fusion.1 = bf16[5,16,32,128]{3,2,1,0:T(8,128)(2,1)} fusion(bf16[1,16,32,128]{3,2,1,0:T(8,128)(2,1)S(1)} %fusion.1, bf16[4,16,32,128]{3,2,1,0:T(8,128)(2,1)S(1)} %get-tuple-element.34), kind=kLoop, calls=%fused_computation.3 | loop fusion | flops 327680 | bytes 1310720 | tf_op jit(solution)/shard_map/concatenate | solution.py:390
  6.6 1.3 %collective-permute-start.1 = (bf16[5,16,32,128]{3,2,1,0:T(8,128)(2,1)}, bf16[5,16,32,128]{3,2,1,0:T(8,128)(2,1)S(1)}, u32[]{:S(2)}, u32[]{:S(2)}) collective-permute-start(bf16[5,16,32,128]{3,2,1,0:T(8,128)(2,1)} %pad_maximum_fusion.1), channel_id=1, source_target_pairs={{1,0},{2,1},{3,2},{4,3},{5,4},{6,5},{7,6},{8,7},{9,8},{10,9},{11,1... | collective-permute-start | bytes 1966088 | tf_op jit(solution)/shard_map/ppermute | solution.py:381
  7.9 0.1 reduce_sum.29
  8.0 0.1 copy.17
  8.1 0.1 copy_divide_fusion.k_ref
  8.2 7.5 %bands_and_turn.1 = (bf16[256,96]{1,0:T(8,128)(2,1)S(1)}, bf16[2,256,256]{2,1,0:T(8,128)(2,1)S(1)}, bf16[2,256,256]{2,1,0:T(8,128)(2,1)S(1)}, bf16[4,256,256]{2,...) custom-call(f32[4,3,31]{2,1,0:T(4,128)S(1)} %copy_divide_fusion.k_re, ...), custom_call_target="tpu_custom_call" | custom-call | flops 1000000000 | bytes 20000000 | tf_op jit(solution)/shard_map/bands_and_turn/pallas_call | solution.py:84
  15.8 7.2 %first_iteration.1 = (f32[32,32,128]{2,1,0:T(8,128)S(1)}, bf16[32,32,128]{2,1,0:T(8,128)(2,1)S(1)}, bf16[4,32,64,128]{3,2,1,0:T(8,128)(2,1)S(1)}) custom-call(bf16[5,512,128]{2,1,0:T(8,128)(2,1)S(1)} %bitcast.25, bf16[5,512,128]{2,1,0:T(8,128)(2,1)S(1)} %bitcast.26, bf16[4,32,32,128]{3,2,1,0:T(8,128)(2,1)S(1)} %get-tuple-element.17.meast_ref, ...), custom_call_target="tpu_custom_call" | custom-call | flops 6000000000 | bytes 8000000 | tf_op jit(solution)/shard_map/first_iteration/pallas_call | solution.py:227
  23.0 1.3 %copy-done.7 = bf16[4,32,64,128]{3,2,1,0:T(8,128)(2,1)} copy-done((bf16[4,32,64,128]{3,2,1,0:T(8,128)(2,1)}, bf16[4,32,64,128]{3,2,1,0:T(8,128)(2,1)S(1)}, u32[]{:S(2)}) %copy-start.7) | copy-done | bytes 2097176
  24.3 0.8 copy-done.9
  25.1 9.3 %collective-permute-start.2 = (bf16[32,32,128]{2,1,0:T(8,128)(2,1)S(1)}, bf16[32,32,128]{2,1,0:T(8,128)(2,1)S(1)}, u32[]{:S(2)}, u32[]{:S(2)}) collective-permute-start(bf16[32,32,128]{2,1,0:T(8,128)(2,1)S(1)} %get-tuple-element.25), channel_id=1, source_target_pairs={{0,1},{1,2},{2,3},{3,4},{4,5},{5,6},{6,7},{7,8},{8,9},{9,10},{10,1... | collective-permute-start | bytes 786440 | tf_op jit(solution)/shard_map/ppermute | solution.py:381
  34.4 1.5 %collective-permute-start.3 = (bf16[32,32,128]{2,1,0:T(8,128)(2,1)S(1)}, bf16[32,32,128]{2,1,0:T(8,128)(2,1)S(1)}, u32[]{:S(2)}, u32[]{:S(2)}) collective-permute-start(bf16[32,32,128]{2,1,0:T(8,128)(2,1)S(1)} %get-tuple-element.25), channel_id=1, source_target_pairs={{1,0},{2,1},{3,2},{4,3},{5,4},{6,5},{7,6},{8,7},{9,8},{10,9},{11,1... | collective-permute-start | bytes 786440 | tf_op jit(solution)/shard_map/ppermute | solution.py:381
  35.9 0.1 reshape.64
  36.0 0.1 pad_bitcast_fusion.2
  36.1 0.1 maximum_bitcast_fusion
  36.2 3.5 %collective-permute-done.3.hi_ref = bf16[32,32,128]{2,1,0:T(8,128)(2,1)S(1)} collective-permute-done((bf16[32,32,128]{2,1,0:T(8,128)(2,1)S(1)}, bf16[32,32,128]{2,1,0:T(8,128)(2,1)S(1)}, u32[]{:S(2)}, u32[]{:S(2)}) %collective-permute-start.3) | collective-permute-done | bytes 262176 | tf_op jit(solution)/shard_map/ppermute | solution.py:381
  39.7 0.9 %copy-done.2 = bf16[2,256,256]{2,1,0:T(8,128)(2,1)S(1)} copy-done((bf16[2,256,256]{2,1,0:T(8,128)(2,1)S(1)}, bf16[2,256,256]{2,1,0:T(8,128)(2,1)}, u32[]{:S(2)}) %copy-start.2) | copy-done | bytes 262168
  40.6 0.9 %copy-done.4 = bf16[2,256,256]{2,1,0:T(8,128)(2,1)S(1)} copy-done((bf16[2,256,256]{2,1,0:T(8,128)(2,1)S(1)}, bf16[2,256,256]{2,1,0:T(8,128)(2,1)}, u32[]{:S(2)}) %copy-start.4) | copy-done | bytes 262168
  41.6 0.9 %copy-done.6 = bf16[192,512]{1,0:T(8,128)(2,1)S(1)} copy-done((bf16[192,512]{1,0:T(8,128)(2,1)S(1)}, bf16[192,512]{1,0:T(8,128)(2,1)}, u32[]{:S(2)}) %copy-start.6) | copy-done | bytes 196632
  42.5 1.6 %copy-done.8 = bf16[4,32,64,128]{3,2,1,0:T(8,128)(2,1)S(1)} copy-done((bf16[4,32,64,128]{3,2,1,0:T(8,128)(2,1)S(1)}, bf16[4,32,64,128]{3,2,1,0:T(8,128)(2,1)}, u32[]{:S(2)}) %copy-start.8) | copy-done | bytes 2097176
  44.1 1.0 %copy-done.10 = f32[32,32,128]{2,1,0:T(8,128)S(1)} copy-done((f32[32,32,128]{2,1,0:T(8,128)S(1)}, f32[32,32,128]{2,1,0:T(8,128)}, u32[]{:S(2)}) %copy-start.10) | copy-done | bytes 524312
  45.1 5.9 %second_iteration.1 = (f32[1024,128]{1,0:T(8,128)}, f32[1088,128]{1,0:T(8,128)S(1)}, f32[16]{0:T(128)S(1)}) custom-call(bf16[32,32,128]{2,1,0:T(8,128)(2,1)S(1)} %collective-permute-done.2.lo_ref, bf16[32,32,128]{2,1,0:T(8,128)(2,1)S(1)} %collective-permute-done.3.hi_ref, bf16[4,32,64,128]{3,2,1,0:T(8,128)(2,1)S(1)} %copy-done.8, ...), custom_call_target="tpu_custom_call" | custom-call | flops 6000000000 | bytes 8000000 | tf_op jit(solution)/shard_map/second_iteration/pallas_call | solution.py:244
  51.1 0.7 copy.19
  51.7 8.4 %all-to-all-start = ((f32[16,1,1]{2,1,0:T(1,128)}), f32[16,1,1]{2,1,0:T(1,128)S(1)}, u32[]{:S(2)}, u32[]{:S(2)}) async-start(f32[16,1,1]{2,1,0:T(1,128)} %copy.19), calls=%async_computation | async-start | bytes 16384 | tf_op jit(solution)/shard_map/all_to_all | solution.py:396
  60.2 0.1 add_convert_fusion.flag_ref
  60.3 6.2 %all-to-all-done = f32[16,1,1]{2,1,0:T(1,128)S(1)} async-done(((f32[16,1,1]{2,1,0:T(1,128)}), f32[16,1,1]{2,1,0:T(1,128)S(1)}, u32[]{:S(2)}, u32[]{:S(2)}) %all-to-all-start) | async-done | bytes 96 | tf_op jit(solution)/shard_map/all_to_all | solution.py:396
  66.5 0.2 reduce.tot_ref
  66.9 12.3 %conv_head.1 = f32[1024,128]{1,0:T(8,128)} custom-call(f32[16]{0:T(128)S(1)} %reduce.tot_ref, f32[2]{0:T(128)S(1)} %add_convert_fusion.flag_ref, f32[1088,128]{1,0:T(8,128)S(1)} %get-tuple-element.31.est_ref, f32[2,16,128]{2,1,0:T(8,128)S(1)} %broadcast_in_dim.4.stem_ref, f32[2,16,128]{2,1,0:T(8,128)S(1)} %broadcast_in_dim.5.head_ref, ...), custom_call_target="tpu_custom_call" | custom-call | flops 4000000000 | bytes 2000000 | tf_op jit(solution)/shard_map/conv_head/pallas_call | solution.py:362
  (30 shorter events, 0.3 us)
Async XLA Ops:
  0.6 1.5 %copy-start = (bf16[4,32,32,128]{3,2,1,0:T(8,128)(2,1)S(1)}, bf16[4,32,32,128]{3,2,1,0:T(8,128)(2,1)}, u32[]{:S(2)}) copy-start(bf16[4,32,32,128]{3,2,1,0:T(8,128)(2,1)} %param.5) | copy-start | bytes 3145732
  2.3 5.6 %copy-start.11 = (f32[4,3,31]{2,0,1:T(4,128)S(1)}, f32[4,3,31]{2,0,1:T(4,128)}, u32[]{:S(2)}) copy-start(f32[4,3,31]{2,0,1:T(4,128)} %param.6) | copy-start | bytes 4468
  3.3 12.4 %collective-permute-start = (bf16[5,16,32,128]{3,2,1,0:T(8,128)(2,1)}, bf16[5,16,32,128]{3,2,1,0:T(8,128)(2,1)S(1)}, u32[]{:S(2)}, u32[]{:S(2)}) collective-permute-start(bf16[5,16,32,128]{3,2,1,0:T(8,128)(2,1)} %pad_maximum_fusion), channel_id=1, source_target_pairs={{0,1},{1,2},{2,3},{3,4},{4,5},{5,6},{6,7},{7,8},{8,9},{9,10},{10,1... | collective-permute-start | bytes 1966088 | tf_op jit(solution)/shard_map/ppermute | solution.py:381
  6.6 9.1 %collective-permute-start.1 = (bf16[5,16,32,128]{3,2,1,0:T(8,128)(2,1)}, bf16[5,16,32,128]{3,2,1,0:T(8,128)(2,1)S(1)}, u32[]{:S(2)}, u32[]{:S(2)}) collective-permute-start(bf16[5,16,32,128]{3,2,1,0:T(8,128)(2,1)} %pad_maximum_fusion.1), channel_id=1, source_target_pairs={{1,0},{2,1},{3,2},{4,3},{5,4},{6,5},{7,6},{8,7},{9,8},{10,9},{11,1... | collective-permute-start | bytes 1966088 | tf_op jit(solution)/shard_map/ppermute | solution.py:381
  15.7 7.3 %copy-start.1 = (bf16[2,256,256]{2,1,0:T(8,128)(2,1)}, bf16[2,256,256]{2,1,0:T(8,128)(2,1)S(1)}, u32[]{:S(2)}) copy-start(bf16[2,256,256]{2,1,0:T(8,128)(2,1)S(1)} %get-tuple-element.20.bz) | copy-start | bytes 786436
  15.7 7.3 %copy-start.3 = (bf16[2,256,256]{2,1,0:T(8,128)(2,1)}, bf16[2,256,256]{2,1,0:T(8,128)(2,1)S(1)}, u32[]{:S(2)}) copy-start(bf16[2,256,256]{2,1,0:T(8,128)(2,1)S(1)} %get-tuple-element.21.bzt) | copy-start | bytes 786436
  15.7 7.3 %copy-start.5 = (bf16[192,512]{1,0:T(8,128)(2,1)}, bf16[192,512]{1,0:T(8,128)(2,1)S(1)}, u32[]{:S(2)}) copy-start(bf16[192,512]{1,0:T(8,128)(2,1)S(1)} %get-tuple-element.28.bxt) | copy-start | bytes 589828
  15.8 20.1 %copy-start.12 = (bf16[432,16]{0,1:T(8,128)(2,1)S(1)}, bf16[432,16]{0,1:T(8,128)(2,1)}, u32[]{:S(2)}) copy-start(bf16[432,16]{0,1:T(8,128)(2,1)} %param.8) | copy-start | bytes 41476
  23.0 1.3 %copy-start.7 = (bf16[4,32,64,128]{3,2,1,0:T(8,128)(2,1)}, bf16[4,32,64,128]{3,2,1,0:T(8,128)(2,1)S(1)}, u32[]{:S(2)}) copy-start(bf16[4,32,64,128]{3,2,1,0:T(8,128)(2,1)S(1)} %get-tuple-element.26.measx_ref) | copy-start | bytes 6291460
  24.3 0.8 %copy-start.9 = (f32[32,32,128]{2,1,0:T(8,128)}, f32[32,32,128]{2,1,0:T(8,128)S(1)}, u32[]{:S(2)}) copy-start(f32[32,32,128]{2,1,0:T(8,128)S(1)} %get-tuple-element.27.est_ref) | copy-start | bytes 1572868
  25.1 11.1 %collective-permute-start.2 = (bf16[32,32,128]{2,1,0:T(8,128)(2,1)S(1)}, bf16[32,32,128]{2,1,0:T(8,128)(2,1)S(1)}, u32[]{:S(2)}, u32[]{:S(2)}) collective-permute-start(bf16[32,32,128]{2,1,0:T(8,128)(2,1)S(1)} %get-tuple-element.25), channel_id=1, source_target_pairs={{0,1},{1,2},{2,3},{3,4},{4,5},{5,6},{6,7},{7,8},{8,9},{9,10},{10,1... | collective-permute-start | bytes 786440 | tf_op jit(solution)/shard_map/ppermute | solution.py:381
  34.4 5.3 %collective-permute-start.3 = (bf16[32,32,128]{2,1,0:T(8,128)(2,1)S(1)}, bf16[32,32,128]{2,1,0:T(8,128)(2,1)S(1)}, u32[]{:S(2)}, u32[]{:S(2)}) collective-permute-start(bf16[32,32,128]{2,1,0:T(8,128)(2,1)S(1)} %get-tuple-element.25), channel_id=1, source_target_pairs={{1,0},{2,1},{3,2},{4,3},{5,4},{6,5},{7,6},{8,7},{9,8},{10,9},{11,1... | collective-permute-start | bytes 786440 | tf_op jit(solution)/shard_map/ppermute | solution.py:381
  39.7 1.0 %copy-start.2 = (bf16[2,256,256]{2,1,0:T(8,128)(2,1)S(1)}, bf16[2,256,256]{2,1,0:T(8,128)(2,1)}, u32[]{:S(2)}) copy-start(bf16[2,256,256]{2,1,0:T(8,128)(2,1)} %copy-done.1) | copy-start | bytes 786436
  40.6 0.9 %copy-start.4 = (bf16[2,256,256]{2,1,0:T(8,128)(2,1)S(1)}, bf16[2,256,256]{2,1,0:T(8,128)(2,1)}, u32[]{:S(2)}) copy-start(bf16[2,256,256]{2,1,0:T(8,128)(2,1)} %copy-done.3) | copy-start | bytes 786436
  41.6 0.9 %copy-start.6 = (bf16[192,512]{1,0:T(8,128)(2,1)S(1)}, bf16[192,512]{1,0:T(8,128)(2,1)}, u32[]{:S(2)}) copy-start(bf16[192,512]{1,0:T(8,128)(2,1)} %copy-done.5) | copy-start | bytes 589828
  42.5 1.6 %copy-start.8 = (bf16[4,32,64,128]{3,2,1,0:T(8,128)(2,1)S(1)}, bf16[4,32,64,128]{3,2,1,0:T(8,128)(2,1)}, u32[]{:S(2)}) copy-start(bf16[4,32,64,128]{3,2,1,0:T(8,128)(2,1)} %copy-done.7) | copy-start | bytes 6291460
  44.1 1.0 %copy-start.10 = (f32[32,32,128]{2,1,0:T(8,128)S(1)}, f32[32,32,128]{2,1,0:T(8,128)}, u32[]{:S(2)}) copy-start(f32[32,32,128]{2,1,0:T(8,128)} %copy-done.9) | copy-start | bytes 1572868
  45.1 21.6 %copy-start.13 = (f32[2,16]{1,0:T(2,128)S(1)}, f32[2,16]{1,0:T(2,128)}, u32[]{:S(2)}) copy-start(f32[2,16]{1,0:T(2,128)} %param.7) | copy-start | bytes 388
  45.1 21.7 %copy-start.14 = (f32[2,16]{1,0:T(2,128)S(1)}, f32[2,16]{1,0:T(2,128)}, u32[]{:S(2)}) copy-start(f32[2,16]{1,0:T(2,128)} %param.9) | copy-start | bytes 388
  51.7 14.8 %all-to-all-start = ((f32[16,1,1]{2,1,0:T(1,128)}), f32[16,1,1]{2,1,0:T(1,128)S(1)}, u32[]{:S(2)}, u32[]{:S(2)}) async-start(f32[16,1,1]{2,1,0:T(1,128)} %copy.19), calls=%async_computation | async-start | bytes 16384 | tf_op jit(solution)/shard_map/all_to_all | solution.py:396

commit v2 on v1

--- a/solution.py
+++ b/solution.py
@@ -93,6 +93,30 @@
     )(kernels, measured.reshape(views, 1024, 128))
 
 
+def message_kernel(meas_ref, up_ref, down_ref):
+    views, rows = meas_ref.shape[0], meas_ref.shape[1] // 2
+    for ref, near, far in ((up_ref, rows, 0), (down_ref, 0, rows)):
+        acc = None
+        for v in range(views):
+            ref[v] = meas_ref[v, near:near + rows, :]
+            m = meas_ref[v, far:far + rows, :].astype(F32)
+            acc = m if acc is None else acc + m
+        ref[views] = (acc * (1.0 / views)).astype(BF16)
+
+
+def message_call(measured):
+    views, rows, _ = measured.shape
+    shape = jax.ShapeDtypeStruct((views + 1, rows // 2, 128), BF16)
+    return pl.pallas_call(
+        message_kernel,
+        out_shape=[shape, shape],
+        in_specs=[VMEM],
+        out_specs=[VMEM, VMEM],
+        compiler_params=pltpu.CompilerParams(vmem_limit_bytes=16 * 2**20),
+        name="halo_messages",
+    )(measured)
+
+
 XN, ZM, YN, XT = 8, 8, 8, 8
 
 
@@ -122,7 +146,11 @@
                 for a in range(2):
                     top = m[:, 8 * a:8 * a + 8, :].reshape(256, 128)
                     at = (2 * h + a) * 128
-                    ratio = jnp.where(top > 0.0, top / q[:, at:at + 128], 0.0)
+                    low = q[:, at:at + 128]
+                    inverse = pl.reciprocal(low, approx=True)
+                    ratio = top * (inverse * (2.0 - low * inverse))
+                    if h in (0, YN // 2 - 1):
+                        ratio = jnp.where(top > 0.0, ratio, 0.0)
                     wide.append(ratio.astype(BF16))
             q = jnp.dot(lyt_ref[v], jnp.concatenate(wide, axis=1), preferred_element_type=F32)
             for h in range(YN // 2):
@@ -175,7 +203,7 @@
         eb_ref[32:64, pl.ds(col, 128)] = est_ref[y].astype(BF16)
         return 0
 
-    lax.fori_loop(0, 32, turn, 0, unroll=2)
+    lax.fori_loop(0, 32, turn, 0, unroll=4)
 
     def finish(y, f, carry):
         e = est_ref[y] * f
@@ -195,7 +223,7 @@
         eb_ref[64:96, pl.ds(col, 128)] = hi_ref[y]
         return 0
 
-    lax.fori_loop(0, 32, fill, 0, unroll=2)
+    lax.fori_loop(0, 32, fill, 0, unroll=4)
 
     def finish(y, f, carry):
         mid = est_ref[y] * f[8:40]
@@ -208,9 +236,7 @@
         return carry + ((mid[0:8] + mid[8:16]) + (mid[16:24] + mid[24:32]))
 
     total = correct(eb_ref, measx_ref, kx, bz, bzt, ly, lyt, bxt, 48, a_ref, b_ref, c_ref, d_ref, finish)
-    whole = jnp.sum(total)
-    for k in range(sum_ref.shape[0]):
-        sum_ref[k] = whole
+    sum_ref[...] = jnp.broadcast_to(jnp.sum(total), sum_ref.shape)
 
 
 SCRATCH = [
@@ -246,10 +272,10 @@
         out_shape=[
             jax.ShapeDtypeStruct((1024, 128), F32),
             jax.ShapeDtypeStruct((34 * 32, 128), F32),
-            jax.ShapeDtypeStruct((bricks,), F32),
+            jax.ShapeDtypeStruct((bricks, 1, 128), F32),
         ],
         in_specs=[VMEM] * 10,
-        out_specs=[VMEM, VMEM, SMEM],
+        out_specs=[VMEM] * 3,
         scratch_shapes=SCRATCH,
         compiler_params=pltpu.CompilerParams(vmem_limit_bytes=32 * 2**20),
         cost_estimate=COST,
@@ -283,19 +309,12 @@
     return parts[0]
 
 
-def conv_kernel(count, tot_ref, flag_ref, est_ref, stem_ref, head_ref, w_ref, out_ref, n_ref, f_ref, p_ref):
+def conv_kernel(count, tot_ref, flag_ref, est_ref, stem_ref, head_ref, w_ref, out_ref, n_ref, f_ref, *sums):
     planes = est_ref.shape[0] // 32
     ch = stem_ref.shape[1]
-    total = tot_ref[0]
-    for k in range(1, tot_ref.shape[0]):
-        total = total + tot_ref[k]
-    scale = count / jnp.full((8, 128), total, jnp.float32)
+    scale = count / jnp.broadcast_to(jnp.sum(tot_ref[...], axis=0), (8, 128))
     lane = lax.broadcasted_iota(jnp.int32, (ch, 128), 1)
     w0, b0 = stem_ref[0], stem_ref[1]
-    keep = [lane > 0, None, lane < 127]
-    wz = [w0 if k is None else jnp.where(k, w0, 0.0) for k in keep]
-    bz = [b0 if k is None else jnp.where(k, b0, 0.0) for k in keep]
-
     blank = jnp.zeros((48, planes * 128), jnp.bfloat16)
     for y in (0, 33, 34):
         f_ref[y * 48:(y + 1) * 48, :] = blank
@@ -305,28 +324,28 @@
         col = pl.multiple_of(e * 128, 128)
         v = est_ref[pl.ds(at, 32), :]
         v = (v.reshape(4, 8, 128) * scale[None]).reshape(32, 128)
-        n_ref[0] = pltpu.roll(v, 1, 1)
-        n_ref[1] = v
-        n_ref[2] = pltpu.roll(v, 127, 1)
+        n_ref[...] = v
         flag = jnp.where(e == 0, flag_ref[0], jnp.where(e == planes - 1, flag_ref[1], 1.0))
-        for dz in range(3):
-            w, b = wz[dz] * flag, bz[dz] * flag
-            for y in range(32):
-                row = jnp.broadcast_to(n_ref[dz, y:y + 1, :], (ch, 128))
-                f = jnp.maximum(w * row + b, 0.0).astype(jnp.bfloat16)
-                f_ref[(y + 1) * 48 + dz * 16:(y + 1) * 48 + dz * 16 + 16, pl.ds(col, 128)] = f
+        w, b = w0 * flag, b0 * flag
+        for y in range(32):
+            row = n_ref[pl.ds(y, ch, stride=0), :]
+            f = jnp.maximum(w * row + b, 0.0).astype(jnp.bfloat16)
+            at = (y + 1) * 48
+            f_ref[at:at + 16, pl.ds(col, 128)] = jnp.where(lane > 0, pltpu.roll(f, 1, 1), jnp.zeros_like(f))
+            f_ref[at + 16:at + 32, pl.ds(col, 128)] = f
+            f_ref[at + 32:at + 48, pl.ds(col, 128)] = jnp.where(lane < 127, pltpu.roll(f, 127, 1), jnp.zeros_like(f))
         return 0
 
-    lax.fori_loop(0, planes, plane, 0)
+    lax.fori_loop(0, planes, plane, 0, unroll=6)
     bias = [head_ref[0, 0:8], head_ref[0, 8:16]]
     gain = [head_ref[1, 0:8], head_ref[1, 8:16]]
     m = YB * ch
 
-    def block(k, _):
-        at = pl.multiple_of(k * (YB * 48), 16)
-        p_ref[...] = jnp.dot(w_ref[...], f_ref[pl.ds(at, (YB + 2) * 48), :], preferred_element_type=jnp.float32)
-        for yo in range(YB):
-            rows = []
+    for k in range(11):
+        p_ref = sums[k % len(sums)]
+        at = k * (YB * 48)
+        p_ref[...] = jnp.dot(w_ref[...], f_ref[at:at + (YB + 2) * 48, :], preferred_element_type=jnp.float32)
+        for yo in range(min(YB, 32 - k * YB)):
             for g in range((planes - 2) // 8):
                 parts = []
                 for o in range(g * 8, g * 8 + 8):
@@ -339,19 +358,7 @@
                         acc = jnp.maximum(acc + bias[h], 0.0) * gain[h]
                         s = acc if s is None else s + acc
                     parts.append(s)
-                rows.append(fold_channels(parts))
-
-            def put():
-                for g, r in enumerate(rows):
-                    out_ref[pl.ds(g * 256 + k * YB + yo, 8, stride=32), :] = r
-
-            if yo == YB - 1:
-                pl.when(k * YB + yo < 32)(put)
-            else:
-                put()
-        return 0
-
-    lax.fori_loop(0, 11, block, 0)
+                out_ref[pl.ds(g * 256 + k * YB + yo, 8, stride=32), :] = fold_channels(parts)
 
 
 def conv_call(totals, flags, head, est, stem, w, count):
@@ -362,13 +369,12 @@
     return pl.pallas_call(
         functools.partial(conv_kernel, count),
         out_shape=jax.ShapeDtypeStruct(((planes - 2) * 32, 128), jnp.float32),
-        in_specs=[smem, smem, vmem, vmem, vmem, vmem],
+        in_specs=[vmem, smem, vmem, vmem, vmem, vmem],
         out_specs=vmem,
         scratch_shapes=[
-            pltpu.VMEM((3, 32, 128), jnp.float32),
+            pltpu.VMEM((32, 128), jnp.float32),
             pltpu.VMEM((35 * 48, planes * 128), jnp.bfloat16),
-            pltpu.VMEM((3 * YB * ch, planes * 128), jnp.float32),
-        ],
+        ] + [pltpu.VMEM((3 * YB * ch, planes * 128), jnp.float32)],
         compiler_params=pltpu.CompilerParams(vmem_limit_bytes=40 * 2**20),
         cost_estimate=pl.CostEstimate(flops=4 * 10**9, bytes_accessed=2 * 10**6, transcendentals=0),
         name="conv_head",
@@ -384,10 +390,8 @@
 def local(measured, psf, stem_params, conv_weight, head_params):
     views, plane_count, row_count, lane_count = measured.shape
     bricks = lax.axis_size("brick")
-    early = jnp.mean(measured[:, :HALO].astype(F32), axis=0, keepdims=True).astype(BF16)
-    late = jnp.mean(measured[:, HALO:].astype(F32), axis=0, keepdims=True).astype(BF16)
-    lo = shifted(jnp.concatenate([measured[:, HALO:], early]), 1)
-    hi = shifted(jnp.concatenate([measured[:, :HALO], late]), -1)
+    up, down = message_call(measured.reshape(views, plane_count * row_count, lane_count))
+    lo, hi = shifted(up, 1), shifted(down, -1)
     kernels = psf / jnp.sum(psf, axis=-1, keepdims=True)
     *mats, bxt, bxt2, meast, est = prep_call(kernels, measured)
     est, estb, measx = first_call(lo, hi, meast, est, mats + [bxt])

time: 79.5 us -> 72.3 us (0.909)
  Pallas kernels: 32.8 us -> 30.3 us
  starting transfers between devices: 22.8 us -> 20.6 us
  local copies, waits for them, and re-layouts: 10.3 us -> 8.49 us
  other arithmetic: 2.58 us -> 1.71 us
    pallas_call x1, Pallas kernels: 12.3 us -> 8.61 us  [conv_call(): pl.pallas_call(functools.partial(conv_kernel, count), out_shape=jax.Shape...]
    ppermute x4, starting transfers between devices: 14.4 us -> 11.8 us  [shifted(): return lax.ppermute(cells, 'brick', pairs)]
    concatenate x2 -> x0, other arithmetic: 1.83 us -> none  [the longest x1 0.93 us: local(): hi = shifted(jnp.concatenate([measured[:, :HALO], late]), -1)]
    slice x1 -> x0, local copies, waits for them, and re-layouts: 1.39 us -> none  [local(): measured[:, :HALO].astype(F32)]
    unnamed x30 -> x26, local copies, waits for them, and re-layouts: 7.74 us -> 8.05 us
  transfers between devices with their start and end apart: 5 -> 5, of which waited for: 2 -> 2; matrix products, arithmetic and copies ran while one was open for 2% -> 3% of each run, Pallas kernels for 9% -> 10%
where the time goes in v2:
time: 72.3 us; the launch traced here: 71.8 us
  Pallas kernels  30.3 us (42%)
  starting transfers between devices  20.6 us (28%)
  waiting for transfers between devices  9.83 us (14%)
  local copies, waits for them, and re-layouts  8.49 us (12%)
  other arithmetic  1.71 us (2%)
  between operations  0.8 us (1%)
    ppermute x4, starting transfers between devices, shifted(): return lax.ppermute(cells, 'brick', pairs)  11.8 us
    all_to_all x1, starting transfers between devices, local(): totals = lax.all_to_all(mine, 'brick', 0, 0, tiled=True)  8.83 us
    pallas_call x1, Pallas kernels, conv_call(): pl.pallas_call(functools.partial(conv_kernel, count), out_shape=jax.Shape...  8.61 us
    unnamed x26, local copies, waits for them, and re-layouts  8.05 us
    pallas_call x1, Pallas kernels, prep_call(): pl.pallas_call(prep_kernel, out_shape=[jax.ShapeDtypeStruct(s, d) for s,...  7.48 us
    pallas_call x1, Pallas kernels, first_call(): pl.pallas_call(first_kernel, out_shape=[jax.ShapeDtypeStruct((32, 32, 128...  7.45 us
    pallas_call x1, Pallas kernels, second_call(): pl.pallas_call(second_kernel, out_shape=[jax.ShapeDtypeStruct((1024, 128)...  6.55 us
    all_to_all x1, waiting for transfers between devices, local(): totals = lax.all_to_all(mine, 'brick', 0, 0, tiled=True)  6.24 us
  transfers between devices with their start and end apart: 5, of which 2 were waited for; matrix products, arithmetic and copies ran while one was open for 3% of the time, Pallas kernels for 10%

profile of v2, /device:TPU:0, one launch (start us, length us, event | category | flops | bytes accessed | tf_op | source)
XLA Modules:
  0.0 71.8 jit_solution(13434919049199055720)
XLA Ops:
  0.6 0.0 copy-start
  0.6 1.2 %copy-done = bf16[4,32,32,128]{3,2,1,0:T(8,128)(2,1)S(1)} copy-done((bf16[4,32,32,128]{3,2,1,0:T(8,128)(2,1)S(1)}, bf16[4,32,32,128]{3,2,1,0:T(8,128)(2,1)}, u32[]{:S(2)}) %copy-start) | copy-done | bytes 1048600
  1.9 0.2 halo_messages.1
  2.0 2.4 %collective-permute-start = (bf16[5,512,128]{2,1,0:T(8,128)(2,1)S(1)}, bf16[5,512,128]{2,1,0:T(8,128)(2,1)S(1)}, u32[]{:S(2)}, u32[]{:S(2)}) collective-permute-start(bf16[5,512,128]{2,1,0:T(8,128)(2,1)S(1)} %get-tuple-element.19), channel_id=1, source_target_pairs={{0,1},{1,2},{2,3},{3,4},{4,5},{5,6},{6,7},{7,8},{8,9},{9,10},{10,1... | collective-permute-start | bytes 1966088 | tf_op jit(solution)/shard_map/ppermute | solution.py:387
  4.5 1.3 %collective-permute-start.1 = (bf16[5,512,128]{2,1,0:T(8,128)(2,1)S(1)}, bf16[5,512,128]{2,1,0:T(8,128)(2,1)S(1)}, u32[]{:S(2)}, u32[]{:S(2)}) collective-permute-start(bf16[5,512,128]{2,1,0:T(8,128)(2,1)S(1)} %get-tuple-element.20), channel_id=1, source_target_pairs={{1,0},{2,1},{3,2},{4,3},{5,4},{6,5},{7,6},{8,7},{9,8},{10,9},{11,1... | collective-permute-start | bytes 1966088 | tf_op jit(solution)/shard_map/ppermute | solution.py:387
  5.8 0.8 %reduce_sum.9 = f32[4,3]{0,1:T(4,128)S(1)} reduce(f32[4,3,31]{2,0,1:T(4,128)} %param.6, f32[]{:T(128)} %constant.2.clone.1), dimensions={2}, to_apply=%region_0.0 | reduce | flops 360 | bytes 1540 | tf_op jit(solution)/shard_map/reduce_sum | solution.py:395
  6.5 0.1 copy.13
  6.6 0.8 %copy_divide_fusion.k_ref = f32[4,3,31]{2,1,0:T(4,128)S(1)} fusion(f32[4,3,31]{2,0,1:T(4,128)} %param.6, f32[4,3]{1,0:T(4,128)S(1)} %copy.13), kind=kLoop, calls=%fused_computation.4 | loop fusion | flops 372 | bytes 3024 | tf_op jit(solution)/shard_map/div | solution.py:395
  7.4 1.2 %copy-done.1 = bf16[4,32,32,128]{3,2,1,0:T(8,128)(2,1)S(1)} copy-done((bf16[4,32,32,128]{3,2,1,0:T(8,128)(2,1)S(1)}, bf16[4,32,32,128]{3,2,1,0:T(8,128)(2,1)}, u32[]{:S(2)}) %copy-start.1) | copy-done | bytes 1048600
  8.6 7.5 %bands_and_turn.1 = (bf16[256,96]{1,0:T(8,128)(2,1)S(1)}, bf16[2,256,256]{2,1,0:T(8,128)(2,1)S(1)}, bf16[2,256,256]{2,1,0:T(8,128)(2,1)S(1)}, bf16[4,256,256]{2,...) custom-call(f32[4,3,31]{2,1,0:T(4,128)S(1)} %copy_divide_fusion.k_re, ...), custom_call_target="tpu_custom_call" | custom-call | flops 1000000000 | bytes 20000000 | tf_op jit(solution)/shard_map/bands_and_turn/pallas_call | solution.py:84
  16.1 0.7 copy-done.6
  16.8 0.0 collective-permute-done.lo_ref
  16.8 0.0 collective-permute-done.1.hi_ref
  16.8 0.0 copy-start.10
  16.8 7.5 %first_iteration.1 = (f32[32,32,128]{2,1,0:T(8,128)S(1)}, bf16[32,32,128]{2,1,0:T(8,128)(2,1)S(1)}, bf16[4,32,64,128]{3,2,1,0:T(8,128)(2,1)S(1)}) custom-call(bf16[5,512,128]{2,1,0:T(8,128)(2,1)S(1)} %collective-permute-done.lo_ref, bf16[5,512,128]{2,1,0:T(8,128)(2,1)S(1)} %collective-permute-done.1.hi_ref, ...), custom_call_target="tpu_custom_call" | custom-call | flops 6000000000 | bytes 8000000 | tf_op jit(solution)/shard_map/first_iteration/pallas_call | solution.py:253
  24.3 1.3 %copy-done.8 = bf16[4,32,64,128]{3,2,1,0:T(8,128)(2,1)} copy-done((bf16[4,32,64,128]{3,2,1,0:T(8,128)(2,1)}, bf16[4,32,64,128]{3,2,1,0:T(8,128)(2,1)S(1)}, u32[]{:S(2)}) %copy-start.8) | copy-done | bytes 2097176
  25.7 6.7 %collective-permute-start.2 = (bf16[32,32,128]{2,1,0:T(8,128)(2,1)S(1)}, bf16[32,32,128]{2,1,0:T(8,128)(2,1)S(1)}, u32[]{:S(2)}, u32[]{:S(2)}) collective-permute-start(bf16[32,32,128]{2,1,0:T(8,128)(2,1)S(1)} %get-tuple-element.29), channel_id=1, source_target_pairs={{0,1},{1,2},{2,3},{3,4},{4,5},{5,6},{6,7},{7,8},{8,9},{9,10},{10,1... | collective-permute-start | bytes 786440 | tf_op jit(solution)/shard_map/ppermute | solution.py:387
  32.3 1.5 %collective-permute-start.3 = (bf16[32,32,128]{2,1,0:T(8,128)(2,1)S(1)}, bf16[32,32,128]{2,1,0:T(8,128)(2,1)S(1)}, u32[]{:S(2)}, u32[]{:S(2)}) collective-permute-start(bf16[32,32,128]{2,1,0:T(8,128)(2,1)S(1)} %get-tuple-element.29), channel_id=1, source_target_pairs={{1,0},{2,1},{3,2},{4,3},{5,4},{6,5},{7,6},{8,7},{9,8},{10,9},{11,1... | collective-permute-start | bytes 786440 | tf_op jit(solution)/shard_map/ppermute | solution.py:387
  33.8 0.1 reshape.25
  33.9 0.1 pad_bitcast_fusion.2
  34.0 0.1 maximum_bitcast_fusion
  34.1 3.6 %collective-permute-done.3.hi_ref = bf16[32,32,128]{2,1,0:T(8,128)(2,1)S(1)} collective-permute-done((bf16[32,32,128]{2,1,0:T(8,128)(2,1)S(1)}, bf16[32,32,128]{2,1,0:T(8,128)(2,1)S(1)}, u32[]{:S(2)}, u32[]{:S(2)}) %collective-permute-start.3) | collective-permute-done | bytes 262176 | tf_op jit(solution)/shard_map/ppermute | solution.py:387
  37.7 1.0 %copy-done.3 = bf16[4,256,256]{2,1,0:T(8,128)(2,1)S(1)} copy-done((bf16[4,256,256]{2,1,0:T(8,128)(2,1)S(1)}, bf16[4,256,256]{2,1,0:T(8,128)(2,1)}, u32[]{:S(2)}) %copy-start.3) | copy-done | bytes 524312
  38.8 0.9 %copy-done.5 = bf16[2,256,256]{2,1,0:T(8,128)(2,1)S(1)} copy-done((bf16[2,256,256]{2,1,0:T(8,128)(2,1)S(1)}, bf16[2,256,256]{2,1,0:T(8,128)(2,1)}, u32[]{:S(2)}) %copy-start.5) | copy-done | bytes 262168
  39.7 1.6 %copy-done.9 = bf16[4,32,64,128]{3,2,1,0:T(8,128)(2,1)S(1)} copy-done((bf16[4,32,64,128]{3,2,1,0:T(8,128)(2,1)S(1)}, bf16[4,32,64,128]{3,2,1,0:T(8,128)(2,1)}, u32[]{:S(2)}) %copy-start.9) | copy-done | bytes 2097176
  41.3 6.6 %second_iteration.1 = (f32[1024,128]{1,0:T(8,128)}, f32[1088,128]{1,0:T(8,128)S(1)}, f32[16,1,128]{2,1,0:T(1,128)}) custom-call(bf16[32,32,128]{2,1,0:T(8,128)(2,1)S(1)} %collective-permute-done.2.lo_ref, bf16[32,32,128]{2,1,0:T(8,128)(2,1)S(1)} %collective-permute-done.3.hi_ref, bf16[4,32,64,128]{3,2,1,0:T(8,128)(2,1)S(1)} %copy-done.9, ...), custom_call_target="tpu_custom_call" | custom-call | flops 6000000000 | bytes 8000000 | tf_op jit(solution)/shard_map/second_iteration/pallas_call | solution.py:270
  47.9 8.8 %all-to-all-start = ((f32[16,1,128]{2,1,0:T(1,128)}), f32[16,1,128]{2,1,0:T(1,128)S(1)}, u32[]{:S(2)}, u32[]{:S(2)}) async-start(f32[16,1,128]{2,1,0:T(1,128)} %get-tuple-element.34), calls=%async_computation | async-start | bytes 16384 | tf_op jit(solution)/shard_map/all_to_all | solution.py:400
  56.7 0.1 add_convert_fusion.flag_ref
  56.8 6.2 %all-to-all-done.tot_ref = f32[16,1,128]{2,1,0:T(1,128)S(1)} async-done(((f32[16,1,128]{2,1,0:T(1,128)}), f32[16,1,128]{2,1,0:T(1,128)S(1)}, u32[]{:S(2)}, u32[]{:S(2)}) %all-to-all-start) | async-done | bytes 8224 | tf_op jit(solution)/shard_map/all_to_all | solution.py:400
  63.0 0.1 broadcast_in_dim.4.stem_ref
  63.1 0.1 broadcast_in_dim.5.head_ref
  63.2 8.6 %conv_head.1 = f32[1024,128]{1,0:T(8,128)} custom-call(f32[16,1,128]{2,1,0:T(1,128)S(1)} %all-to-all-done.tot_ref, f32[2]{0:T(128)S(1)} %add_convert_fusion.flag_ref, f32[1088,128]{1,0:T(8,128)S(1)} %get-tuple-element.35.est_ref, f32[2,16,128]{2,1,0:T(8,128)S(1)} %broadcast_in_dim.4.stem_ref, f32[2,16,128]{2,1,0:T(8,128)S(1)} %broadcast_in_dim.5.head_ref, ...), custom_call_target="tpu_custom_call" | custom-call | flops 4000000000 | bytes 2000000 | tf_op jit(solution)/shard_map/conv_head/pallas_call | solution.py:369
  (19 shorter events, 0.0 us)
Async XLA Ops:
  0.6 1.2 %copy-start = (bf16[4,32,32,128]{3,2,1,0:T(8,128)(2,1)S(1)}, bf16[4,32,32,128]{3,2,1,0:T(8,128)(2,1)}, u32[]{:S(2)}) copy-start(bf16[4,32,32,128]{3,2,1,0:T(8,128)(2,1)} %param.5) | copy-start | bytes 3145732
  2.0 14.8 %collective-permute-start = (bf16[5,512,128]{2,1,0:T(8,128)(2,1)S(1)}, bf16[5,512,128]{2,1,0:T(8,128)(2,1)S(1)}, u32[]{:S(2)}, u32[]{:S(2)}) collective-permute-start(bf16[5,512,128]{2,1,0:T(8,128)(2,1)S(1)} %get-tuple-element.19), channel_id=1, source_target_pairs={{0,1},{1,2},{2,3},{3,4},{4,5},{5,6},{6,7},{7,8},{8,9},{9,10},{10,1... | collective-permute-start | bytes 1966088 | tf_op jit(solution)/shard_map/ppermute | solution.py:387
  4.5 12.4 %collective-permute-start.1 = (bf16[5,512,128]{2,1,0:T(8,128)(2,1)S(1)}, bf16[5,512,128]{2,1,0:T(8,128)(2,1)S(1)}, u32[]{:S(2)}, u32[]{:S(2)}) collective-permute-start(bf16[5,512,128]{2,1,0:T(8,128)(2,1)S(1)} %get-tuple-element.20), channel_id=1, source_target_pairs={{1,0},{2,1},{3,2},{4,3},{5,4},{6,5},{7,6},{8,7},{9,8},{10,9},{11,1... | collective-permute-start | bytes 1966088 | tf_op jit(solution)/shard_map/ppermute | solution.py:387
  7.4 1.2 %copy-start.1 = (bf16[4,32,32,128]{3,2,1,0:T(8,128)(2,1)S(1)}, bf16[4,32,32,128]{3,2,1,0:T(8,128)(2,1)}, u32[]{:S(2)}) copy-start(bf16[4,32,32,128]{3,2,1,0:T(8,128)(2,1)} %param.5) | copy-start | bytes 3145732
  16.1 0.7 copy-start.6
  16.8 7.5 %copy-start.2 = (bf16[4,256,256]{2,1,0:T(8,128)(2,1)}, bf16[4,256,256]{2,1,0:T(8,128)(2,1)S(1)}, u32[]{:S(2)}) copy-start(bf16[4,256,256]{2,1,0:T(8,128)(2,1)S(1)} %get-tuple-element.27.lyt) | copy-start | bytes 1572868
  16.8 7.5 %copy-start.4 = (bf16[2,256,256]{2,1,0:T(8,128)(2,1)}, bf16[2,256,256]{2,1,0:T(8,128)(2,1)S(1)}, u32[]{:S(2)}) copy-start(bf16[2,256,256]{2,1,0:T(8,128)(2,1)S(1)} %get-tuple-element.25.bzt) | copy-start | bytes 786436
  16.8 17.0 %copy-start.10 = (bf16[432,16]{0,1:T(8,128)(2,1)S(1)}, bf16[432,16]{0,1:T(8,128)(2,1)}, u32[]{:S(2)}) copy-start(bf16[432,16]{0,1:T(8,128)(2,1)} %param.8) | copy-start | bytes 41476
  16.8 20.9 %copy-start.7 = (bf16[192,512]{1,0:T(8,128)(2,1)S(1)}, bf16[192,512]{1,0:T(8,128)(2,1)}, u32[]{:S(2)}) copy-start(bf16[192,512]{1,0:T(8,128)(2,1)} %copy-done.6) | copy-start | bytes 589828
  24.3 1.3 %copy-start.8 = (bf16[4,32,64,128]{3,2,1,0:T(8,128)(2,1)}, bf16[4,32,64,128]{3,2,1,0:T(8,128)(2,1)S(1)}, u32[]{:S(2)}) copy-start(bf16[4,32,64,128]{3,2,1,0:T(8,128)(2,1)S(1)} %get-tuple-element.30.measx_ref) | copy-start | bytes 6291460
  25.7 8.5 %collective-permute-start.2 = (bf16[32,32,128]{2,1,0:T(8,128)(2,1)S(1)}, bf16[32,32,128]{2,1,0:T(8,128)(2,1)S(1)}, u32[]{:S(2)}, u32[]{:S(2)}) collective-permute-start(bf16[32,32,128]{2,1,0:T(8,128)(2,1)S(1)} %get-tuple-element.29), channel_id=1, source_target_pairs={{0,1},{1,2},{2,3},{3,4},{4,5},{5,6},{6,7},{7,8},{8,9},{9,10},{10,1... | collective-permute-start | bytes 786440 | tf_op jit(solution)/shard_map/ppermute | solution.py:387
  32.3 5.4 %collective-permute-start.3 = (bf16[32,32,128]{2,1,0:T(8,128)(2,1)S(1)}, bf16[32,32,128]{2,1,0:T(8,128)(2,1)S(1)}, u32[]{:S(2)}, u32[]{:S(2)}) collective-permute-start(bf16[32,32,128]{2,1,0:T(8,128)(2,1)S(1)} %get-tuple-element.29), channel_id=1, source_target_pairs={{1,0},{2,1},{3,2},{4,3},{5,4},{6,5},{7,6},{8,7},{9,8},{10,9},{11,1... | collective-permute-start | bytes 786440 | tf_op jit(solution)/shard_map/ppermute | solution.py:387
  37.7 1.0 %copy-start.3 = (bf16[4,256,256]{2,1,0:T(8,128)(2,1)S(1)}, bf16[4,256,256]{2,1,0:T(8,128)(2,1)}, u32[]{:S(2)}) copy-start(bf16[4,256,256]{2,1,0:T(8,128)(2,1)} %copy-done.2) | copy-start | bytes 1572868
  38.8 0.9 %copy-start.5 = (bf16[2,256,256]{2,1,0:T(8,128)(2,1)S(1)}, bf16[2,256,256]{2,1,0:T(8,128)(2,1)}, u32[]{:S(2)}) copy-start(bf16[2,256,256]{2,1,0:T(8,128)(2,1)} %copy-done.4) | copy-start | bytes 786436
  39.7 1.6 %copy-start.9 = (bf16[4,32,64,128]{3,2,1,0:T(8,128)(2,1)S(1)}, bf16[4,32,64,128]{3,2,1,0:T(8,128)(2,1)}, u32[]{:S(2)}) copy-start(bf16[4,32,64,128]{3,2,1,0:T(8,128)(2,1)} %copy-done.8) | copy-start | bytes 6291460
  41.3 21.7 %copy-start.11 = (f32[2,16]{1,0:T(2,128)S(1)}, f32[2,16]{1,0:T(2,128)}, u32[]{:S(2)}) copy-start(f32[2,16]{1,0:T(2,128)} %param.7) | copy-start | bytes 388
  41.3 21.8 %copy-start.12 = (f32[2,16]{1,0:T(2,128)S(1)}, f32[2,16]{1,0:T(2,128)}, u32[]{:S(2)}) copy-start(f32[2,16]{1,0:T(2,128)} %param.9) | copy-start | bytes 388
  47.9 15.2 %all-to-all-start = ((f32[16,1,128]{2,1,0:T(1,128)}), f32[16,1,128]{2,1,0:T(1,128)S(1)}, u32[]{:S(2)}, u32[]{:S(2)}) async-start(f32[16,1,128]{2,1,0:T(1,128)} %get-tuple-element.34), calls=%async_computation | async-start | bytes 16384 | tf_op jit(solution)/shard_map/all_to_all | solution.py:400

commit v3 on v2

--- a/solution.py
+++ b/solution.py
@@ -24,7 +24,7 @@
     return out
 
 
-def prep_kernel(k_ref, meas_ref, kx_ref, bz_ref, bzt_ref, ly_ref, lyt_ref, bxt_ref, bxt2_ref, meast_ref, est_ref, nat_ref):
+def prep_kernel(k_ref, meas_ref, w_ref, stem_ref, head_ref, flag_ref, kx_ref, bz_ref, bzt_ref, ly_ref, lyt_ref, bxt_ref, bxt2_ref, meast_ref, est_ref, nat_ref):
     views = k_ref.shape[0]
     reach = (k_ref.shape[2] - 1) // 2
     r, c = iotas((64, 96))
@@ -68,7 +68,7 @@
     lax.fori_loop(0, 32, turn, 0)
 
 
-def prep_call(kernels, measured):
+def prep_call(kernels, measured, later):
     views = measured.shape[0]
     out = [
         ((views * 64, 96), BF16),
@@ -84,13 +84,13 @@
     return pl.pallas_call(
         prep_kernel,
         out_shape=[jax.ShapeDtypeStruct(s, d) for s, d in out],
-        in_specs=[SMEM, VMEM],
+        in_specs=[SMEM, VMEM] + [pl.BlockSpec(memory_space=pl.ANY)] * 4,
         out_specs=[VMEM] * len(out),
         scratch_shapes=[pltpu.VMEM((views, 1024, 128), F32)],
         compiler_params=pltpu.CompilerParams(vmem_limit_bytes=16 * 2**20),
         cost_estimate=pl.CostEstimate(flops=10**9, bytes_accessed=20 * 10**6, transcendentals=0),
         name="bands_and_turn",
-    )(kernels, measured.reshape(views, 1024, 128))
+    )(kernels, measured.reshape(views, 1024, 128), *later)
 
 
 def message_kernel(meas_ref, up_ref, down_ref):
@@ -361,7 +361,8 @@
                 out_ref[pl.ds(g * 256 + k * YB + yo, 8, stride=32), :] = fold_channels(parts)
 
 
-def conv_call(totals, flags, head, est, stem, w, count):
+def conv_call(totals, est, later, count):
+    w, stem, head, flags = later
     planes = est.shape[0] // 32
     ch = head.shape[1]
     smem = pl.BlockSpec(memory_space=pltpu.SMEM)
@@ -378,7 +379,7 @@
         compiler_params=pltpu.CompilerParams(vmem_limit_bytes=40 * 2**20),
         cost_estimate=pl.CostEstimate(flops=4 * 10**9, bytes_accessed=2 * 10**6, transcendentals=0),
         name="conv_head",
-    )(totals, flags, est, stem, jnp.broadcast_to(head[:, :, None], (2, ch, 128)), w)
+    )(totals, flags, est, stem, head, w)
 
 
 def shifted(cells, step):
@@ -393,16 +394,18 @@
     up, down = message_call(measured.reshape(views, plane_count * row_count, lane_count))
     lo, hi = shifted(up, 1), shifted(down, -1)
     kernels = psf / jnp.sum(psf, axis=-1, keepdims=True)
-    *mats, bxt, bxt2, meast, est = prep_call(kernels, measured)
+    place = lax.axis_index("brick")
+    flags = jnp.stack([place > 0, place < bricks - 1]).astype(F32)
+    stem = jnp.broadcast_to(stem_params[:, :, None], stem_params.shape + (lane_count,))
+    head = jnp.broadcast_to(head_params[:, :, None], head_params.shape + (lane_count,))
+    later = (conv_matrix(conv_weight), stem, head, flags)
+    *mats, bxt, bxt2, meast, est = prep_call(kernels, measured, later)
     est, estb, measx = first_call(lo, hi, meast, est, mats + [bxt])
     lo, hi = shifted(estb, 1), shifted(estb, -1)
     out, ext, mine = second_call(lo, hi, measx, est, mats + [bxt2], bricks)
     totals = lax.all_to_all(mine, "brick", 0, 0, tiled=True)
-    place = lax.axis_index("brick")
-    flags = jnp.stack([place > 0, place < bricks - 1]).astype(F32)
-    stem = jnp.broadcast_to(stem_params[:, :, None], stem_params.shape + (lane_count,))
     cell_count = bricks * plane_count * row_count * lane_count
-    logits = conv_call(totals, flags, head_params, ext, stem, conv_matrix(conv_weight), float(cell_count))
+    logits = conv_call(totals, ext, later, float(cell_count))
     shape = (plane_count, row_count, lane_count)
     return out.reshape(shape), logits.reshape(shape)
 

time: 72.3 us -> 68.1 us (0.942)
  blocking collectives: 0 us -> 18 us
  starting transfers between devices: 20.6 us -> 10.9 us
  waiting for transfers between devices: 9.83 us -> 0.95 us
  local copies, waits for them, and re-layouts: 8.49 us -> 4.97 us
    all_to_all x0 -> x1, blocking collectives: none -> 18 us  [local(): totals = lax.all_to_all(mine, 'brick', 0, 0, tiled=True)]
    all_to_all x1 -> x0, starting transfers between devices: 8.83 us -> none  [local(): totals = lax.all_to_all(mine, 'brick', 0, 0, tiled=True)]
    all_to_all x1 -> x0, waiting for transfers between devices: 6.24 us -> none  [local(): totals = lax.all_to_all(mine, 'brick', 0, 0, tiled=True)]
    unnamed x26 -> x4, local copies, waits for them, and re-layouts: 8.05 us -> 2.45 us
    ppermute x4, waiting for transfers between devices: 3.6 us -> 0.95 us  [shifted(): return lax.ppermute(cells, 'brick', pairs)]
    ppermute x4, starting transfers between devices: 11.8 us -> 10.9 us  [shifted(): return lax.ppermute(cells, 'brick', pairs)]
  transfers between devices with their start and end apart: 5 -> 4, of which waited for: 2 -> 1; matrix products, arithmetic and copies ran while one was open for 3% -> 6% of each run, Pallas kernels for 10% -> 11%
where the time goes in v3:
time: 68.1 us; the launch traced here: 67.6 us
  Pallas kernels  30.3 us (44%)
  blocking collectives  18 us (26%)
  starting transfers between devices  10.9 us (16%)
  local copies, waits for them, and re-layouts  4.97 us (7%)
  other arithmetic  1.71 us (3%)
  waiting for transfers between devices  0.95 us (1%)
  between operations  0.74 us (1%)
    all_to_all x1, blocking collectives, local(): totals = lax.all_to_all(mine, 'brick', 0, 0, tiled=True)  18 us
    ppermute x4, starting transfers between devices, shifted(): return lax.ppermute(cells, 'brick', pairs)  10.9 us
    pallas_call x1, Pallas kernels, conv_call(): pl.pallas_call(functools.partial(conv_kernel, count), out_shape=jax.Shape...  8.65 us
    pallas_call x1, Pallas kernels, prep_call(): pl.pallas_call(prep_kernel, out_shape=[jax.ShapeDtypeStruct(s, d) for s,...  7.48 us
    pallas_call x1, Pallas kernels, first_call(): pl.pallas_call(first_kernel, out_shape=[jax.ShapeDtypeStruct((32, 32, 128...  7.44 us
    pallas_call x1, Pallas kernels, second_call(): pl.pallas_call(second_kernel, out_shape=[jax.ShapeDtypeStruct((1024, 128)...  6.55 us
    unnamed x4, local copies, waits for them, and re-layouts  2.45 us
  transfers between devices with their start and end apart: 4, of which 1 were waited for; matrix products, arithmetic and copies ran while one was open for 6% of the time, Pallas kernels for 11%

profile of v3, /device:TPU:0, one launch (start us, length us, event | category | flops | bytes accessed | tf_op | source)
XLA Modules:
  0.0 67.6 jit_solution(15232503931848666438)
XLA Ops:
  0.6 0.0 copy-start
  0.6 1.2 %copy-done = bf16[4,32,32,128]{3,2,1,0:T(8,128)(2,1)S(1)} copy-done((bf16[4,32,32,128]{3,2,1,0:T(8,128)(2,1)S(1)}, bf16[4,32,32,128]{3,2,1,0:T(8,128)(2,1)}, u32[]{:S(2)}) %copy-start) | copy-done | bytes 1048600
  1.9 0.2 halo_messages.1
  2.0 2.4 %collective-permute-start = (bf16[5,512,128]{2,1,0:T(8,128)(2,1)S(1)}, bf16[5,512,128]{2,1,0:T(8,128)(2,1)S(1)}, u32[]{:S(2)}, u32[]{:S(2)}) collective-permute-start(bf16[5,512,128]{2,1,0:T(8,128)(2,1)S(1)} %get-tuple-element.19), channel_id=1, source_target_pairs={{0,1},{1,2},{2,3},{3,4},{4,5},{5,6},{6,7},{7,8},{8,9},{9,10},{10,1... | collective-permute-start | bytes 1966088 | tf_op jit(solution)/shard_map/ppermute | solution.py:388
  4.5 1.3 %collective-permute-start.1 = (bf16[5,512,128]{2,1,0:T(8,128)(2,1)S(1)}, bf16[5,512,128]{2,1,0:T(8,128)(2,1)S(1)}, u32[]{:S(2)}, u32[]{:S(2)}) collective-permute-start(bf16[5,512,128]{2,1,0:T(8,128)(2,1)S(1)} %get-tuple-element.20), channel_id=1, source_target_pairs={{1,0},{2,1},{3,2},{4,3},{5,4},{6,5},{7,6},{8,7},{9,8},{10,9},{11,1... | collective-permute-start | bytes 1966088 | tf_op jit(solution)/shard_map/ppermute | solution.py:388
  5.8 0.8 %reduce_sum.9 = f32[4,3]{0,1:T(4,128)S(1)} reduce(f32[4,3,31]{2,0,1:T(4,128)} %param.6, f32[]{:T(128)} %constant.2.clone.1), dimensions={2}, to_apply=%region_0.0 | reduce | flops 360 | bytes 1540 | tf_op jit(solution)/shard_map/reduce_sum | solution.py:396
  6.5 0.1 copy.13
  6.6 0.8 %reshape.24 = bf16[16,3,144]{2,1,0:T(4,128)(2,1)S(1)} reshape(bf16[16,432]{1,0:T(8,128)(2,1)} %bitcast.19) | data formatting | bytes 27648 | tf_op jit(solution)/shard_map/reshape | solution.py:290
  7.4 0.1 pad_bitcast_fusion.2
  7.6 0.1 maximum_bitcast_fusion
  7.7 0.1 add_convert_fusion.flag_ref
  7.7 0.8 %copy_divide_fusion.k_ref = f32[4,3,31]{2,1,0:T(4,128)S(1)} fusion(f32[4,3,31]{2,0,1:T(4,128)} %param.6, f32[4,3]{1,0:T(4,128)S(1)} %copy.13), kind=kLoop, calls=%fused_computation.4 | loop fusion | flops 372 | bytes 3024 | tf_op jit(solution)/shard_map/div | solution.py:396
  8.5 0.8 %broadcast_in_dim.4.stem_ref = f32[2,16,128]{2,1,0:T(8,128)S(1)} broadcast(f32[2,16]{1,0:T(2,128)} %param.7), dimensions={0,1} | broadcast | bytes 16512 | tf_op jit(solution)/shard_map/broadcast_in_dim | solution.py:399
  9.3 0.7 %broadcast_in_dim.5.head_ref = f32[2,16,128]{2,1,0:T(8,128)S(1)} broadcast(f32[2,16]{1,0:T(2,128)} %param.9), dimensions={0,1} | broadcast | bytes 16512 | tf_op jit(solution)/shard_map/broadcast_in_dim | solution.py:400
  10.0 0.0 copy-start.1
  10.0 1.2 %copy-done.1 = bf16[4,32,32,128]{3,2,1,0:T(8,128)(2,1)S(1)} copy-done((bf16[4,32,32,128]{3,2,1,0:T(8,128)(2,1)S(1)}, bf16[4,32,32,128]{3,2,1,0:T(8,128)(2,1)}, u32[]{:S(2)}) %copy-start.1) | copy-done | bytes 1048600
  11.2 7.5 %bands_and_turn.1 = (bf16[256,96]{1,0:T(8,128)(2,1)S(1)}, bf16[2,256,256]{2,1,0:T(8,128)(2,1)S(1)}, bf16[2,256,256]{2,1,0:T(8,128)(2,1)S(1)}, bf16[4,256,256]{2,...) custom-call(f32[4,3,31]{2,1,0:T(4,128)S(1)} %copy_divide_fusion.k_re, ...), custom_call_target="tpu_custom_call" | custom-call | flops 1000000000 | bytes 20000000 | tf_op jit(solution)/shard_map/bands_and_turn/pallas_call | solution.py:84
  18.7 0.0 collective-permute-done.lo_ref
  18.7 0.0 collective-permute-done.1.hi_ref
  18.8 7.4 %first_iteration.1 = (f32[32,32,128]{2,1,0:T(8,128)S(1)}, bf16[32,32,128]{2,1,0:T(8,128)(2,1)S(1)}, bf16[4,32,64,128]{3,2,1,0:T(8,128)(2,1)S(1)}) custom-call(bf16[5,512,128]{2,1,0:T(8,128)(2,1)S(1)} %collective-permute-done.lo_ref, bf16[5,512,128]{2,1,0:T(8,128)(2,1)S(1)} %collective-permute-done.1.hi_ref, ...), custom_call_target="tpu_custom_call" | custom-call | flops 6000000000 | bytes 8000000 | tf_op jit(solution)/shard_map/first_iteration/pallas_call | solution.py:253
  26.2 1.3 %collective-permute-start.3 = (bf16[32,32,128]{2,1,0:T(8,128)(2,1)S(1)}, bf16[32,32,128]{2,1,0:T(8,128)(2,1)S(1)}, u32[]{:S(2)}, u32[]{:S(2)}) collective-permute-start(bf16[32,32,128]{2,1,0:T(8,128)(2,1)S(1)} %get-tuple-element.29), channel_id=1, source_target_pairs={{1,0},{2,1},{3,2},{4,3},{5,4},{6,5},{7,6},{8,7},{9,8},{10,9},{11,1... | collective-permute-start | bytes 786440 | tf_op jit(solution)/shard_map/ppermute | solution.py:388
  27.5 6.0 %collective-permute-start.2 = (bf16[32,32,128]{2,1,0:T(8,128)(2,1)S(1)}, bf16[32,32,128]{2,1,0:T(8,128)(2,1)S(1)}, u32[]{:S(2)}, u32[]{:S(2)}) collective-permute-start(bf16[32,32,128]{2,1,0:T(8,128)(2,1)S(1)} %get-tuple-element.29), channel_id=1, source_target_pairs={{0,1},{1,2},{2,3},{3,4},{4,5},{5,6},{6,7},{7,8},{8,9},{9,10},{10,1... | collective-permute-start | bytes 786440 | tf_op jit(solution)/shard_map/ppermute | solution.py:388
  33.5 0.0 collective-permute-done.3.hi_ref
  33.5 0.9 %collective-permute-done.2.lo_ref = bf16[32,32,128]{2,1,0:T(8,128)(2,1)S(1)} collective-permute-done((bf16[32,32,128]{2,1,0:T(8,128)(2,1)S(1)}, bf16[32,32,128]{2,1,0:T(8,128)(2,1)S(1)}, u32[]{:S(2)}, u32[]{:S(2)}) %collective-permute-start.2) | collective-permute-done | bytes 262176 | tf_op jit(solution)/shard_map/ppermute | solution.py:388
  34.4 6.6 %second_iteration.1 = (f32[1024,128]{1,0:T(8,128)}, f32[1088,128]{1,0:T(8,128)S(1)}, f32[16,1,128]{2,1,0:T(1,128)S(1)}) custom-call(bf16[32,32,128]{2,1,0:T(8,128)(2,1)S(1)} %collective-permute-done.2.lo_ref, bf16[32,32,128]{2,1,0:T(8,128)(2,1)S(1)} %collective-permute-done.3.hi_ref, bf16[4,32,64,128]{3,2,1,0:T(8,128)(2,1)S(1)} %get-tuple-element.30.measx_ref, ...), custom_call_target="tpu_custom_call" | custom-call | flops 6000000000 | bytes 8000000 | tf_op jit(solution)/shard_map/second_iteration/pallas_call | solution.py:270
  41.0 18.0 %all_to_all.5.tot_ref = f32[16,1,128]{2,1,0:T(1,128)S(1)} all-to-all(f32[16,1,128]{2,1,0:T(1,128)S(1)} %get-tuple-element.34), channel_id=1, replica_groups=mesh['span'=2,'brick'=16] {'brick'}, dimensions={0} | all-to-all | bytes 16384 | tf_op jit(solution)/shard_map/all_to_all | solution.py:406
  59.0 8.6 %conv_head.1 = f32[1024,128]{1,0:T(8,128)} custom-call(f32[16,1,128]{2,1,0:T(1,128)S(1)} %all_to_all.5.tot_ref, f32[2]{0:T(128)S(1)} %add_convert_fusion.flag_ref, f32[1088,128]{1,0:T(8,128)S(1)} %get-tuple-element.35.est_ref, f32[2,16,128]{2,1,0:T(8,128)S(1)} %broadcast_in_dim.4.stem_ref, f32[2,16,128]{2,1,0:T(8,128)S(1)} %broadcast_in_dim.5.head_ref, ...), custom_call_target="tpu_custom_call" | custom-call | flops 4000000000 | bytes 2000000 | tf_op jit(solution)/shard_map/conv_head/pallas_call | solution.py:370
  (1 shorter events, 0.0 us)
Async XLA Ops:
  0.6 1.2 %copy-start = (bf16[4,32,32,128]{3,2,1,0:T(8,128)(2,1)S(1)}, bf16[4,32,32,128]{3,2,1,0:T(8,128)(2,1)}, u32[]{:S(2)}) copy-start(bf16[4,32,32,128]{3,2,1,0:T(8,128)(2,1)} %param.5) | copy-start | bytes 3145732
  2.0 16.7 %collective-permute-start = (bf16[5,512,128]{2,1,0:T(8,128)(2,1)S(1)}, bf16[5,512,128]{2,1,0:T(8,128)(2,1)S(1)}, u32[]{:S(2)}, u32[]{:S(2)}) collective-permute-start(bf16[5,512,128]{2,1,0:T(8,128)(2,1)S(1)} %get-tuple-element.19), channel_id=1, source_target_pairs={{0,1},{1,2},{2,3},{3,4},{4,5},{5,6},{6,7},{7,8},{8,9},{9,10},{10,1... | collective-permute-start | bytes 1966088 | tf_op jit(solution)/shard_map/ppermute | solution.py:388
  4.5 14.3 %collective-permute-start.1 = (bf16[5,512,128]{2,1,0:T(8,128)(2,1)S(1)}, bf16[5,512,128]{2,1,0:T(8,128)(2,1)S(1)}, u32[]{:S(2)}, u32[]{:S(2)}) collective-permute-start(bf16[5,512,128]{2,1,0:T(8,128)(2,1)S(1)} %get-tuple-element.20), channel_id=1, source_target_pairs={{1,0},{2,1},{3,2},{4,3},{5,4},{6,5},{7,6},{8,7},{9,8},{10,9},{11,1... | collective-permute-start | bytes 1966088 | tf_op jit(solution)/shard_map/ppermute | solution.py:388
  10.0 1.2 %copy-start.1 = (bf16[4,32,32,128]{3,2,1,0:T(8,128)(2,1)S(1)}, bf16[4,32,32,128]{3,2,1,0:T(8,128)(2,1)}, u32[]{:S(2)}) copy-start(bf16[4,32,32,128]{3,2,1,0:T(8,128)(2,1)} %param.5) | copy-start | bytes 3145732
  26.2 7.3 %collective-permute-start.3 = (bf16[32,32,128]{2,1,0:T(8,128)(2,1)S(1)}, bf16[32,32,128]{2,1,0:T(8,128)(2,1)S(1)}, u32[]{:S(2)}, u32[]{:S(2)}) collective-permute-start(bf16[32,32,128]{2,1,0:T(8,128)(2,1)S(1)} %get-tuple-element.29), channel_id=1, source_target_pairs={{1,0},{2,1},{3,2},{4,3},{5,4},{6,5},{7,6},{8,7},{9,8},{10,9},{11,1... | collective-permute-start | bytes 786440 | tf_op jit(solution)/shard_map/ppermute | solution.py:388
  27.5 6.9 %collective-permute-start.2 = (bf16[32,32,128]{2,1,0:T(8,128)(2,1)S(1)}, bf16[32,32,128]{2,1,0:T(8,128)(2,1)S(1)}, u32[]{:S(2)}, u32[]{:S(2)}) collective-permute-start(bf16[32,32,128]{2,1,0:T(8,128)(2,1)S(1)} %get-tuple-element.29), channel_id=1, source_target_pairs={{0,1},{1,2},{2,3},{3,4},{4,5},{5,6},{6,7},{7,8},{8,9},{9,10},{10,1... | collective-permute-start | bytes 786440 | tf_op jit(solution)/shard_map/ppermute | solution.py:388

commit v4 on v3

--- a/solution.py
+++ b/solution.py
@@ -117,7 +117,7 @@
     )(measured)
 
 
-XN, ZM, YN, XT = 8, 8, 8, 8
+XN, ZM, YN, XT = 8, 8, 2, 8
 
 
 def correct(eb_ref, meas, kx_ref, bz_ref, bzt_ref, ly_ref, lyt_ref, bxt_ref, rows, a_ref, b_ref, c_ref, d_ref, finish):
@@ -149,7 +149,7 @@
                     low = q[:, at:at + 128]
                     inverse = pl.reciprocal(low, approx=True)
                     ratio = top * (inverse * (2.0 - low * inverse))
-                    if h in (0, YN // 2 - 1):
+                    if not HALO <= x0 + 16 * h < 64 - HALO:
                         ratio = jnp.where(top > 0.0, ratio, 0.0)
                     wide.append(ratio.astype(BF16))
             q = jnp.dot(lyt_ref[v], jnp.concatenate(wide, axis=1), preferred_element_type=F32)
@@ -336,7 +336,7 @@
             f_ref[at + 32:at + 48, pl.ds(col, 128)] = jnp.where(lane < 127, pltpu.roll(f, 127, 1), jnp.zeros_like(f))
         return 0
 
-    lax.fori_loop(0, planes, plane, 0, unroll=6)
+    lax.fori_loop(0, planes, plane, 0, unroll=17)
     bias = [head_ref[0, 0:8], head_ref[0, 8:16]]
     gain = [head_ref[1, 0:8], head_ref[1, 8:16]]
     m = YB * ch

time: 68.1 us -> 66.4 us (0.975)
  Pallas kernels: 30.3 us -> 28.6 us
    pallas_call x1, Pallas kernels: 7.44 us -> 6.74 us  [first_call(): pl.pallas_call(first_kernel, out_shape=[jax.ShapeDtypeStruct((32, 32, 128...]
where the time goes in v4:
time: 66.4 us; the launch traced here: 65.9 us
  Pallas kernels  28.6 us (43%)
  blocking collectives  18 us (27%)
  starting transfers between devices  10.9 us (16%)
  local copies, waits for them, and re-layouts  4.97 us (7%)
  other arithmetic  1.71 us (3%)
  waiting for transfers between devices  0.95 us (1%)
  between operations  0.74 us (1%)
    all_to_all x1, blocking collectives, local(): totals = lax.all_to_all(mine, 'brick', 0, 0, tiled=True)  18 us
    ppermute x4, starting transfers between devices, shifted(): return lax.ppermute(cells, 'brick', pairs)  10.9 us
    pallas_call x1, Pallas kernels, conv_call(): pl.pallas_call(functools.partial(conv_kernel, count), out_shape=jax.Shape...  8.1 us
    pallas_call x1, Pallas kernels, prep_call(): pl.pallas_call(prep_kernel, out_shape=[jax.ShapeDtypeStruct(s, d) for s,...  7.48 us
    pallas_call x1, Pallas kernels, first_call(): pl.pallas_call(first_kernel, out_shape=[jax.ShapeDtypeStruct((32, 32, 128...  6.74 us
    pallas_call x1, Pallas kernels, second_call(): pl.pallas_call(second_kernel, out_shape=[jax.ShapeDtypeStruct((1024, 128)...  6.06 us
    unnamed x4, local copies, waits for them, and re-layouts  2.45 us
  transfers between devices with their start and end apart: 4, of which 1 were waited for; matrix products, arithmetic and copies ran while one was open for 6% of the time, Pallas kernels for 11%

profile of v4, /device:TPU:0, one launch (start us, length us, event | category | flops | bytes accessed | tf_op | source)
XLA Modules:
  0.0 65.9 jit_solution(1833664468553451354)
XLA Ops:
  0.6 0.0 copy-start
  0.6 1.2 %copy-done = bf16[4,32,32,128]{3,2,1,0:T(8,128)(2,1)S(1)} copy-done((bf16[4,32,32,128]{3,2,1,0:T(8,128)(2,1)S(1)}, bf16[4,32,32,128]{3,2,1,0:T(8,128)(2,1)}, u32[]{:S(2)}) %copy-start) | copy-done | bytes 1048600
  1.9 0.2 halo_messages.1
  2.0 2.4 %collective-permute-start = (bf16[5,512,128]{2,1,0:T(8,128)(2,1)S(1)}, bf16[5,512,128]{2,1,0:T(8,128)(2,1)S(1)}, u32[]{:S(2)}, u32[]{:S(2)}) collective-permute-start(bf16[5,512,128]{2,1,0:T(8,128)(2,1)S(1)} %get-tuple-element.19), channel_id=1, source_target_pairs={{0,1},{1,2},{2,3},{3,4},{4,5},{5,6},{6,7},{7,8},{8,9},{9,10},{10,1... | collective-permute-start | bytes 1966088 | tf_op jit(solution)/shard_map/ppermute | solution.py:388
  4.5 1.3 %collective-permute-start.1 = (bf16[5,512,128]{2,1,0:T(8,128)(2,1)S(1)}, bf16[5,512,128]{2,1,0:T(8,128)(2,1)S(1)}, u32[]{:S(2)}, u32[]{:S(2)}) collective-permute-start(bf16[5,512,128]{2,1,0:T(8,128)(2,1)S(1)} %get-tuple-element.20), channel_id=1, source_target_pairs={{1,0},{2,1},{3,2},{4,3},{5,4},{6,5},{7,6},{8,7},{9,8},{10,9},{11,1... | collective-permute-start | bytes 1966088 | tf_op jit(solution)/shard_map/ppermute | solution.py:388
  5.8 0.8 %reduce_sum.9 = f32[4,3]{0,1:T(4,128)S(1)} reduce(f32[4,3,31]{2,0,1:T(4,128)} %param.6, f32[]{:T(128)} %constant.2.clone.1), dimensions={2}, to_apply=%region_0.0 | reduce | flops 360 | bytes 1540 | tf_op jit(solution)/shard_map/reduce_sum | solution.py:396
  6.5 0.1 copy.13
  6.6 0.8 %reshape.24 = bf16[16,3,144]{2,1,0:T(4,128)(2,1)S(1)} reshape(bf16[16,432]{1,0:T(8,128)(2,1)} %bitcast.19) | data formatting | bytes 27648 | tf_op jit(solution)/shard_map/reshape | solution.py:290
  7.4 0.1 pad_bitcast_fusion.2
  7.6 0.1 maximum_bitcast_fusion
  7.7 0.1 add_convert_fusion.flag_ref
  7.7 0.8 %copy_divide_fusion.k_ref = f32[4,3,31]{2,1,0:T(4,128)S(1)} fusion(f32[4,3,31]{2,0,1:T(4,128)} %param.6, f32[4,3]{1,0:T(4,128)S(1)} %copy.13), kind=kLoop, calls=%fused_computation.4 | loop fusion | flops 372 | bytes 3024 | tf_op jit(solution)/shard_map/div | solution.py:396
  8.5 0.8 %broadcast_in_dim.4.stem_ref = f32[2,16,128]{2,1,0:T(8,128)S(1)} broadcast(f32[2,16]{1,0:T(2,128)} %param.7), dimensions={0,1} | broadcast | bytes 16512 | tf_op jit(solution)/shard_map/broadcast_in_dim | solution.py:399
  9.3 0.7 %broadcast_in_dim.5.head_ref = f32[2,16,128]{2,1,0:T(8,128)S(1)} broadcast(f32[2,16]{1,0:T(2,128)} %param.9), dimensions={0,1} | broadcast | bytes 16512 | tf_op jit(solution)/shard_map/broadcast_in_dim | solution.py:400
  10.0 0.0 copy-start.1
  10.0 1.2 %copy-done.1 = bf16[4,32,32,128]{3,2,1,0:T(8,128)(2,1)S(1)} copy-done((bf16[4,32,32,128]{3,2,1,0:T(8,128)(2,1)S(1)}, bf16[4,32,32,128]{3,2,1,0:T(8,128)(2,1)}, u32[]{:S(2)}) %copy-start.1) | copy-done | bytes 1048600
  11.2 7.5 %bands_and_turn.1 = (bf16[256,96]{1,0:T(8,128)(2,1)S(1)}, bf16[2,256,256]{2,1,0:T(8,128)(2,1)S(1)}, bf16[2,256,256]{2,1,0:T(8,128)(2,1)S(1)}, bf16[4,256,256]{2,...) custom-call(f32[4,3,31]{2,1,0:T(4,128)S(1)} %copy_divide_fusion.k_re, ...), custom_call_target="tpu_custom_call" | custom-call | flops 1000000000 | bytes 20000000 | tf_op jit(solution)/shard_map/bands_and_turn/pallas_call | solution.py:84
  18.7 0.0 collective-permute-done.lo_ref
  18.7 0.0 collective-permute-done.1.hi_ref
  18.8 6.7 %first_iteration.1 = (f32[32,32,128]{2,1,0:T(8,128)S(1)}, bf16[32,32,128]{2,1,0:T(8,128)(2,1)S(1)}, bf16[4,32,64,128]{3,2,1,0:T(8,128)(2,1)S(1)}) custom-call(bf16[5,512,128]{2,1,0:T(8,128)(2,1)S(1)} %collective-permute-done.lo_ref, bf16[5,512,128]{2,1,0:T(8,128)(2,1)S(1)} %collective-permute-done.1.hi_ref, ...), custom_call_target="tpu_custom_call" | custom-call | flops 6000000000 | bytes 8000000 | tf_op jit(solution)/shard_map/first_iteration/pallas_call | solution.py:253
  25.5 1.3 %collective-permute-start.3 = (bf16[32,32,128]{2,1,0:T(8,128)(2,1)S(1)}, bf16[32,32,128]{2,1,0:T(8,128)(2,1)S(1)}, u32[]{:S(2)}, u32[]{:S(2)}) collective-permute-start(bf16[32,32,128]{2,1,0:T(8,128)(2,1)S(1)} %get-tuple-element.29), channel_id=1, source_target_pairs={{1,0},{2,1},{3,2},{4,3},{5,4},{6,5},{7,6},{8,7},{9,8},{10,9},{11,1... | collective-permute-start | bytes 786440 | tf_op jit(solution)/shard_map/ppermute | solution.py:388
  26.8 6.0 %collective-permute-start.2 = (bf16[32,32,128]{2,1,0:T(8,128)(2,1)S(1)}, bf16[32,32,128]{2,1,0:T(8,128)(2,1)S(1)}, u32[]{:S(2)}, u32[]{:S(2)}) collective-permute-start(bf16[32,32,128]{2,1,0:T(8,128)(2,1)S(1)} %get-tuple-element.29), channel_id=1, source_target_pairs={{0,1},{1,2},{2,3},{3,4},{4,5},{5,6},{6,7},{7,8},{8,9},{9,10},{10,1... | collective-permute-start | bytes 786440 | tf_op jit(solution)/shard_map/ppermute | solution.py:388
  32.8 0.0 collective-permute-done.3.hi_ref
  32.8 0.9 %collective-permute-done.2.lo_ref = bf16[32,32,128]{2,1,0:T(8,128)(2,1)S(1)} collective-permute-done((bf16[32,32,128]{2,1,0:T(8,128)(2,1)S(1)}, bf16[32,32,128]{2,1,0:T(8,128)(2,1)S(1)}, u32[]{:S(2)}, u32[]{:S(2)}) %collective-permute-start.2) | collective-permute-done | bytes 262176 | tf_op jit(solution)/shard_map/ppermute | solution.py:388
  33.7 6.1 %second_iteration.1 = (f32[1024,128]{1,0:T(8,128)}, f32[1088,128]{1,0:T(8,128)S(1)}, f32[16,1,128]{2,1,0:T(1,128)S(1)}) custom-call(bf16[32,32,128]{2,1,0:T(8,128)(2,1)S(1)} %collective-permute-done.2.lo_ref, bf16[32,32,128]{2,1,0:T(8,128)(2,1)S(1)} %collective-permute-done.3.hi_ref, bf16[4,32,64,128]{3,2,1,0:T(8,128)(2,1)S(1)} %get-tuple-element.30.measx_ref, ...), custom_call_target="tpu_custom_call" | custom-call | flops 6000000000 | bytes 8000000 | tf_op jit(solution)/shard_map/second_iteration/pallas_call | solution.py:270
  39.8 18.0 %all_to_all.5.tot_ref = f32[16,1,128]{2,1,0:T(1,128)S(1)} all-to-all(f32[16,1,128]{2,1,0:T(1,128)S(1)} %get-tuple-element.34), channel_id=1, replica_groups=mesh['span'=2,'brick'=16] {'brick'}, dimensions={0} | all-to-all | bytes 16384 | tf_op jit(solution)/shard_map/all_to_all | solution.py:406
  57.8 8.1 %conv_head.1 = f32[1024,128]{1,0:T(8,128)} custom-call(f32[16,1,128]{2,1,0:T(1,128)S(1)} %all_to_all.5.tot_ref, f32[2]{0:T(128)S(1)} %add_convert_fusion.flag_ref, f32[1088,128]{1,0:T(8,128)S(1)} %get-tuple-element.35.est_ref, f32[2,16,128]{2,1,0:T(8,128)S(1)} %broadcast_in_dim.4.stem_ref, f32[2,16,128]{2,1,0:T(8,128)S(1)} %broadcast_in_dim.5.head_ref, ...), custom_call_target="tpu_custom_call" | custom-call | flops 4000000000 | bytes 2000000 | tf_op jit(solution)/shard_map/conv_head/pallas_call | solution.py:370
  (1 shorter events, 0.0 us)
Async XLA Ops:
  0.6 1.2 %copy-start = (bf16[4,32,32,128]{3,2,1,0:T(8,128)(2,1)S(1)}, bf16[4,32,32,128]{3,2,1,0:T(8,128)(2,1)}, u32[]{:S(2)}) copy-start(bf16[4,32,32,128]{3,2,1,0:T(8,128)(2,1)} %param.5) | copy-start | bytes 3145732
  2.0 16.7 %collective-permute-start = (bf16[5,512,128]{2,1,0:T(8,128)(2,1)S(1)}, bf16[5,512,128]{2,1,0:T(8,128)(2,1)S(1)}, u32[]{:S(2)}, u32[]{:S(2)}) collective-permute-start(bf16[5,512,128]{2,1,0:T(8,128)(2,1)S(1)} %get-tuple-element.19), channel_id=1, source_target_pairs={{0,1},{1,2},{2,3},{3,4},{4,5},{5,6},{6,7},{7,8},{8,9},{9,10},{10,1... | collective-permute-start | bytes 1966088 | tf_op jit(solution)/shard_map/ppermute | solution.py:388
  4.5 14.3 %collective-permute-start.1 = (bf16[5,512,128]{2,1,0:T(8,128)(2,1)S(1)}, bf16[5,512,128]{2,1,0:T(8,128)(2,1)S(1)}, u32[]{:S(2)}, u32[]{:S(2)}) collective-permute-start(bf16[5,512,128]{2,1,0:T(8,128)(2,1)S(1)} %get-tuple-element.20), channel_id=1, source_target_pairs={{1,0},{2,1},{3,2},{4,3},{5,4},{6,5},{7,6},{8,7},{9,8},{10,9},{11,1... | collective-permute-start | bytes 1966088 | tf_op jit(solution)/shard_map/ppermute | solution.py:388
  10.0 1.2 %copy-start.1 = (bf16[4,32,32,128]{3,2,1,0:T(8,128)(2,1)S(1)}, bf16[4,32,32,128]{3,2,1,0:T(8,128)(2,1)}, u32[]{:S(2)}) copy-start(bf16[4,32,32,128]{3,2,1,0:T(8,128)(2,1)} %param.5) | copy-start | bytes 3145732
  25.5 7.3 %collective-permute-start.3 = (bf16[32,32,128]{2,1,0:T(8,128)(2,1)S(1)}, bf16[32,32,128]{2,1,0:T(8,128)(2,1)S(1)}, u32[]{:S(2)}, u32[]{:S(2)}) collective-permute-start(bf16[32,32,128]{2,1,0:T(8,128)(2,1)S(1)} %get-tuple-element.29), channel_id=1, source_target_pairs={{1,0},{2,1},{3,2},{4,3},{5,4},{6,5},{7,6},{8,7},{9,8},{10,9},{11,1... | collective-permute-start | bytes 786440 | tf_op jit(solution)/shard_map/ppermute | solution.py:388
  26.8 6.9 %collective-permute-start.2 = (bf16[32,32,128]{2,1,0:T(8,128)(2,1)S(1)}, bf16[32,32,128]{2,1,0:T(8,128)(2,1)S(1)}, u32[]{:S(2)}, u32[]{:S(2)}) collective-permute-start(bf16[32,32,128]{2,1,0:T(8,128)(2,1)S(1)} %get-tuple-element.29), channel_id=1, source_target_pairs={{0,1},{1,2},{2,3},{3,4},{4,5},{5,6},{6,7},{7,8},{8,9},{9,10},{10,1... | collective-permute-start | bytes 786440 | tf_op jit(solution)/shard_map/ppermute | solution.py:388

commit v5 on v4

--- a/solution.py
+++ b/solution.py
@@ -214,7 +214,7 @@
     correct(eb_ref, measx_ref, kx, bz, bzt, ly, lyt, bxt, 32, a_ref, b_ref, c_ref, d_ref, finish)
 
 
-def second_kernel(lo_ref, hi_ref, measx_ref, est_ref, kx, bz, bzt, ly, lyt, bxt, out_ref, ext_ref, sum_ref,
+def second_kernel(lo_ref, hi_ref, measx_ref, est_ref, kx, bz, bzt, ly, lyt, bxt, ext_ref, sum_ref,
                   eb_ref, a_ref, b_ref, c_ref, d_ref):
     def fill(y, _):
         col = pl.multiple_of(y * 128, 128)
@@ -229,7 +229,6 @@
         mid = est_ref[y] * f[8:40]
         before = lo_ref[y, 16:32, :].astype(F32)[8:16] * f[0:8]
         after = hi_ref[y, 0:16, :].astype(F32)[0:8] * f[40:48]
-        out_ref[pl.ds(y, 32, stride=32), :] = mid
         ext_ref[pl.ds(32 + y, 32, stride=32), :] = mid
         ext_ref[pl.ds(y, 1), :] = before[7:8]
         ext_ref[pl.ds(33 * 32 + y, 1), :] = after[0:1]
@@ -270,12 +269,11 @@
     return pl.pallas_call(
         second_kernel,
         out_shape=[
-            jax.ShapeDtypeStruct((1024, 128), F32),
             jax.ShapeDtypeStruct((34 * 32, 128), F32),
             jax.ShapeDtypeStruct((bricks, 1, 128), F32),
         ],
         in_specs=[VMEM] * 10,
-        out_specs=[VMEM] * 3,
+        out_specs=[VMEM] * 2,
         scratch_shapes=SCRATCH,
         compiler_params=pltpu.CompilerParams(vmem_limit_bytes=32 * 2**20),
         cost_estimate=COST,
@@ -309,9 +307,11 @@
     return parts[0]
 
 
-def conv_kernel(count, tot_ref, flag_ref, est_ref, stem_ref, head_ref, w_ref, out_ref, n_ref, f_ref, *sums):
+def conv_kernel(count, tot_ref, flag_ref, est_ref, stem_ref, head_ref, w_ref, out_ref, copy_ref, n_ref, f_ref, sem, *sums):
     planes = est_ref.shape[0] // 32
     ch = stem_ref.shape[1]
+    copy = pltpu.make_async_copy(est_ref.at[pl.ds(32, (planes - 2) * 32)], copy_ref, sem)
+    copy.start()
     scale = count / jnp.broadcast_to(jnp.sum(tot_ref[...], axis=0), (8, 128))
     lane = lax.broadcasted_iota(jnp.int32, (ch, 128), 1)
     w0, b0 = stem_ref[0], stem_ref[1]
@@ -359,6 +359,7 @@
                         s = acc if s is None else s + acc
                     parts.append(s)
                 out_ref[pl.ds(g * 256 + k * YB + yo, 8, stride=32), :] = fold_channels(parts)
+    copy.wait()
 
 
 def conv_call(totals, est, later, count):
@@ -369,12 +370,13 @@
     vmem = pl.BlockSpec(memory_space=pltpu.VMEM)
     return pl.pallas_call(
         functools.partial(conv_kernel, count),
-        out_shape=jax.ShapeDtypeStruct(((planes - 2) * 32, 128), jnp.float32),
+        out_shape=[jax.ShapeDtypeStruct(((planes - 2) * 32, 128), jnp.float32)] * 2,
         in_specs=[vmem, smem, vmem, vmem, vmem, vmem],
-        out_specs=vmem,
+        out_specs=[vmem, pl.BlockSpec(memory_space=pl.ANY)],
         scratch_shapes=[
             pltpu.VMEM((32, 128), jnp.float32),
             pltpu.VMEM((35 * 48, planes * 128), jnp.bfloat16),
+            pltpu.SemaphoreType.DMA(()),
         ] + [pltpu.VMEM((3 * YB * ch, planes * 128), jnp.float32)],
         compiler_params=pltpu.CompilerParams(vmem_limit_bytes=40 * 2**20),
         cost_estimate=pl.CostEstimate(flops=4 * 10**9, bytes_accessed=2 * 10**6, transcendentals=0),
@@ -402,10 +404,10 @@
     *mats, bxt, bxt2, meast, est = prep_call(kernels, measured, later)
     est, estb, measx = first_call(lo, hi, meast, est, mats + [bxt])
     lo, hi = shifted(estb, 1), shifted(estb, -1)
-    out, ext, mine = second_call(lo, hi, measx, est, mats + [bxt2], bricks)
+    ext, mine = second_call(lo, hi, measx, est, mats + [bxt2], bricks)
     totals = lax.all_to_all(mine, "brick", 0, 0, tiled=True)
     cell_count = bricks * plane_count * row_count * lane_count
-    logits = conv_call(totals, ext, later, float(cell_count))
+    logits, out = conv_call(totals, ext, later, float(cell_count))
     shape = (plane_count, row_count, lane_count)
     return out.reshape(shape), logits.reshape(shape)
 

time: 66.4 us -> 65.3 us (0.983)
  Pallas kernels: 28.6 us -> 27.4 us
    pallas_call x2, Pallas kernels: 14.2 us -> 13 us  [the longest x1 8.11 us: conv_call(): pl.pallas_call(functools.partial(conv_kernel, count), out_shape=[jax.Shap...]
  transfers between devices with their start and end apart: 4 -> 4, of which waited for: 1 -> 1; matrix products, arithmetic and copies ran while one was open for 6% -> 7% of each run, Pallas kernels for 11% -> 12%
where the time goes in v5:
time: 65.3 us; the launch traced here: 64.9 us
  Pallas kernels  27.4 us (42%)
  blocking collectives  18 us (28%)
  starting transfers between devices  10.9 us (17%)
  local copies, waits for them, and re-layouts  4.97 us (8%)
  other arithmetic  1.71 us (3%)
  waiting for transfers between devices  0.95 us (1%)
  between operations  0.91 us (1%)
    all_to_all x1, blocking collectives, local(): totals = lax.all_to_all(mine, 'brick', 0, 0, tiled=True)  18 us
    ppermute x4, starting transfers between devices, shifted(): return lax.ppermute(cells, 'brick', pairs)  10.9 us
    pallas_call x1, Pallas kernels, conv_call(): pl.pallas_call(functools.partial(conv_kernel, count), out_shape=[jax.Shap...  8.11 us
    pallas_call x1, Pallas kernels, prep_call(): pl.pallas_call(prep_kernel, out_shape=[jax.ShapeDtypeStruct(s, d) for s,...  7.48 us
    pallas_call x1, Pallas kernels, first_call(): pl.pallas_call(first_kernel, out_shape=[jax.ShapeDtypeStruct((32, 32, 128...  6.74 us
    pallas_call x1, Pallas kernels, second_call(): pl.pallas_call(second_kernel, out_shape=[jax.ShapeDtypeStruct((34 * 32, 1...  4.84 us
    unnamed x4, local copies, waits for them, and re-layouts  2.45 us
  transfers between devices with their start and end apart: 4, of which 1 were waited for; matrix products, arithmetic and copies ran while one was open for 7% of the time, Pallas kernels for 12%

profile of v5, /device:TPU:0, one launch (start us, length us, event | category | flops | bytes accessed | tf_op | source)
XLA Modules:
  0.0 64.9 jit_solution(237781303123543574)
XLA Ops:
  0.6 0.0 copy-start
  0.6 1.2 %copy-done = bf16[4,32,32,128]{3,2,1,0:T(8,128)(2,1)S(1)} copy-done((bf16[4,32,32,128]{3,2,1,0:T(8,128)(2,1)S(1)}, bf16[4,32,32,128]{3,2,1,0:T(8,128)(2,1)}, u32[]{:S(2)}) %copy-start) | copy-done | bytes 1048600
  1.9 0.2 halo_messages.1
  2.0 2.4 %collective-permute-start = (bf16[5,512,128]{2,1,0:T(8,128)(2,1)S(1)}, bf16[5,512,128]{2,1,0:T(8,128)(2,1)S(1)}, u32[]{:S(2)}, u32[]{:S(2)}) collective-permute-start(bf16[5,512,128]{2,1,0:T(8,128)(2,1)S(1)} %get-tuple-element.20), channel_id=1, source_target_pairs={{0,1},{1,2},{2,3},{3,4},{4,5},{5,6},{6,7},{7,8},{8,9},{9,10},{10,1... | collective-permute-start | bytes 1966088 | tf_op jit(solution)/shard_map/ppermute | solution.py:390
  4.5 1.3 %collective-permute-start.1 = (bf16[5,512,128]{2,1,0:T(8,128)(2,1)S(1)}, bf16[5,512,128]{2,1,0:T(8,128)(2,1)S(1)}, u32[]{:S(2)}, u32[]{:S(2)}) collective-permute-start(bf16[5,512,128]{2,1,0:T(8,128)(2,1)S(1)} %get-tuple-element.21), channel_id=1, source_target_pairs={{1,0},{2,1},{3,2},{4,3},{5,4},{6,5},{7,6},{8,7},{9,8},{10,9},{11,1... | collective-permute-start | bytes 1966088 | tf_op jit(solution)/shard_map/ppermute | solution.py:390
  5.8 0.8 %reduce_sum.9 = f32[4,3]{0,1:T(4,128)S(1)} reduce(f32[4,3,31]{2,0,1:T(4,128)} %param.6, f32[]{:T(128)} %constant.2.clone.1), dimensions={2}, to_apply=%region_0.0 | reduce | flops 360 | bytes 1540 | tf_op jit(solution)/shard_map/reduce_sum | solution.py:398
  6.5 0.1 copy.13
  6.6 0.8 %reshape.24 = bf16[16,3,144]{2,1,0:T(4,128)(2,1)S(1)} reshape(bf16[16,432]{1,0:T(8,128)(2,1)} %bitcast.19) | data formatting | bytes 27648 | tf_op jit(solution)/shard_map/reshape | solution.py:288
  7.4 0.1 pad_bitcast_fusion.2
  7.6 0.1 maximum_bitcast_fusion
  7.7 0.1 add_convert_fusion.flag_ref
  7.7 0.8 %copy_divide_fusion.k_ref = f32[4,3,31]{2,1,0:T(4,128)S(1)} fusion(f32[4,3,31]{2,0,1:T(4,128)} %param.6, f32[4,3]{1,0:T(4,128)S(1)} %copy.13), kind=kLoop, calls=%fused_computation.4 | loop fusion | flops 372 | bytes 3024 | tf_op jit(solution)/shard_map/div | solution.py:398
  8.5 0.8 %broadcast_in_dim.4.stem_ref = f32[2,16,128]{2,1,0:T(8,128)S(1)} broadcast(f32[2,16]{1,0:T(2,128)} %param.7), dimensions={0,1} | broadcast | bytes 16512 | tf_op jit(solution)/shard_map/broadcast_in_dim | solution.py:401
  9.3 0.7 %broadcast_in_dim.5.head_ref = f32[2,16,128]{2,1,0:T(8,128)S(1)} broadcast(f32[2,16]{1,0:T(2,128)} %param.9), dimensions={0,1} | broadcast | bytes 16512 | tf_op jit(solution)/shard_map/broadcast_in_dim | solution.py:402
  10.0 0.0 copy-start.1
  10.0 1.2 %copy-done.1 = bf16[4,32,32,128]{3,2,1,0:T(8,128)(2,1)S(1)} copy-done((bf16[4,32,32,128]{3,2,1,0:T(8,128)(2,1)S(1)}, bf16[4,32,32,128]{3,2,1,0:T(8,128)(2,1)}, u32[]{:S(2)}) %copy-start.1) | copy-done | bytes 1048600
  11.2 7.5 %bands_and_turn.1 = (bf16[256,96]{1,0:T(8,128)(2,1)S(1)}, bf16[2,256,256]{2,1,0:T(8,128)(2,1)S(1)}, bf16[2,256,256]{2,1,0:T(8,128)(2,1)S(1)}, bf16[4,256,256]{2,...) custom-call(f32[4,3,31]{2,1,0:T(4,128)S(1)} %copy_divide_fusion.k_re, ...), custom_call_target="tpu_custom_call" | custom-call | flops 1000000000 | bytes 20000000 | tf_op jit(solution)/shard_map/bands_and_turn/pallas_call | solution.py:84
  18.7 0.0 collective-permute-done.lo_ref
  18.7 0.0 collective-permute-done.1.hi_ref
  18.8 6.7 %first_iteration.1 = (f32[32,32,128]{2,1,0:T(8,128)S(1)}, bf16[32,32,128]{2,1,0:T(8,128)(2,1)S(1)}, bf16[4,32,64,128]{3,2,1,0:T(8,128)(2,1)S(1)}) custom-call(bf16[5,512,128]{2,1,0:T(8,128)(2,1)S(1)} %collective-permute-done.lo_ref, bf16[5,512,128]{2,1,0:T(8,128)(2,1)S(1)} %collective-permute-done.1.hi_ref, ...), custom_call_target="tpu_custom_call" | custom-call | flops 6000000000 | bytes 8000000 | tf_op jit(solution)/shard_map/first_iteration/pallas_call | solution.py:252
  25.5 1.3 %collective-permute-start.3 = (bf16[32,32,128]{2,1,0:T(8,128)(2,1)S(1)}, bf16[32,32,128]{2,1,0:T(8,128)(2,1)S(1)}, u32[]{:S(2)}, u32[]{:S(2)}) collective-permute-start(bf16[32,32,128]{2,1,0:T(8,128)(2,1)S(1)} %get-tuple-element.30), channel_id=1, source_target_pairs={{1,0},{2,1},{3,2},{4,3},{5,4},{6,5},{7,6},{8,7},{9,8},{10,9},{11,1... | collective-permute-start | bytes 786440 | tf_op jit(solution)/shard_map/ppermute | solution.py:390
  26.8 6.0 %collective-permute-start.2 = (bf16[32,32,128]{2,1,0:T(8,128)(2,1)S(1)}, bf16[32,32,128]{2,1,0:T(8,128)(2,1)S(1)}, u32[]{:S(2)}, u32[]{:S(2)}) collective-permute-start(bf16[32,32,128]{2,1,0:T(8,128)(2,1)S(1)} %get-tuple-element.30), channel_id=1, source_target_pairs={{0,1},{1,2},{2,3},{3,4},{4,5},{5,6},{6,7},{7,8},{8,9},{9,10},{10,1... | collective-permute-start | bytes 786440 | tf_op jit(solution)/shard_map/ppermute | solution.py:390
  32.8 0.0 collective-permute-done.3.hi_ref
  32.8 0.9 %collective-permute-done.2.lo_ref = bf16[32,32,128]{2,1,0:T(8,128)(2,1)S(1)} collective-permute-done((bf16[32,32,128]{2,1,0:T(8,128)(2,1)S(1)}, bf16[32,32,128]{2,1,0:T(8,128)(2,1)S(1)}, u32[]{:S(2)}, u32[]{:S(2)}) %collective-permute-start.2) | collective-permute-done | bytes 262176 | tf_op jit(solution)/shard_map/ppermute | solution.py:390
  33.7 4.8 %second_iteration.1 = (f32[1088,128]{1,0:T(8,128)S(1)}, f32[16,1,128]{2,1,0:T(1,128)S(1)}) custom-call(bf16[32,32,128]{2,1,0:T(8,128)(2,1)S(1)} %collective-permute-done.2.lo_ref, bf16[32,32,128]{2,1,0:T(8,128)(2,1)S(1)} %collective-permute-done.3.hi_ref, bf16[4,32,64,128]{3,2,1,0:T(8,128)(2,1)S(1)} %get-tuple-element.31.measx_ref, ...), custom_call_target="tpu_custom_call" | custom-call | flops 6000000000 | bytes 8000000 | tf_op jit(solution)/shard_map/second_iteration/pallas_call | solution.py:269
  38.5 18.0 %all_to_all.5.tot_ref = f32[16,1,128]{2,1,0:T(1,128)S(1)} all-to-all(f32[16,1,128]{2,1,0:T(1,128)S(1)} %get-tuple-element.34), channel_id=1, replica_groups=mesh['span'=2,'brick'=16] {'brick'}, dimensions={0} | all-to-all | bytes 16384 | tf_op jit(solution)/shard_map/all_to_all | solution.py:408
  56.6 8.1 %conv_head.1 = (f32[1024,128]{1,0:T(8,128)}, f32[1024,128]{1,0:T(8,128)}) custom-call(f32[16,1,128]{2,1,0:T(1,128)S(1)} %all_to_all.5.tot_ref, f32[2]{0:T(128)S(1)} %add_convert_fusion.flag_ref, f32[1088,128]{1,0:T(8,128)S(1)} %get-tuple-element.35.est_ref, f32[2,16,128]{2,1,0:T(8,128)S(1)} %broadcast_in_dim.4.stem_ref, ...), custom_call_target="tpu_custom_call" | custom-call | flops 4000000000 | bytes 2000000 | tf_op jit(solution)/shard_map/conv_head/pallas_call | solution.py:371
  (1 shorter events, 0.0 us)
Async XLA Ops:
  0.6 1.2 %copy-start = (bf16[4,32,32,128]{3,2,1,0:T(8,128)(2,1)S(1)}, bf16[4,32,32,128]{3,2,1,0:T(8,128)(2,1)}, u32[]{:S(2)}) copy-start(bf16[4,32,32,128]{3,2,1,0:T(8,128)(2,1)} %param.5) | copy-start | bytes 3145732
  2.0 16.7 %collective-permute-start = (bf16[5,512,128]{2,1,0:T(8,128)(2,1)S(1)}, bf16[5,512,128]{2,1,0:T(8,128)(2,1)S(1)}, u32[]{:S(2)}, u32[]{:S(2)}) collective-permute-start(bf16[5,512,128]{2,1,0:T(8,128)(2,1)S(1)} %get-tuple-element.20), channel_id=1, source_target_pairs={{0,1},{1,2},{2,3},{3,4},{4,5},{5,6},{6,7},{7,8},{8,9},{9,10},{10,1... | collective-permute-start | bytes 1966088 | tf_op jit(solution)/shard_map/ppermute | solution.py:390
  4.5 14.3 %collective-permute-start.1 = (bf16[5,512,128]{2,1,0:T(8,128)(2,1)S(1)}, bf16[5,512,128]{2,1,0:T(8,128)(2,1)S(1)}, u32[]{:S(2)}, u32[]{:S(2)}) collective-permute-start(bf16[5,512,128]{2,1,0:T(8,128)(2,1)S(1)} %get-tuple-element.21), channel_id=1, source_target_pairs={{1,0},{2,1},{3,2},{4,3},{5,4},{6,5},{7,6},{8,7},{9,8},{10,9},{11,1... | collective-permute-start | bytes 1966088 | tf_op jit(solution)/shard_map/ppermute | solution.py:390
  10.0 1.2 %copy-start.1 = (bf16[4,32,32,128]{3,2,1,0:T(8,128)(2,1)S(1)}, bf16[4,32,32,128]{3,2,1,0:T(8,128)(2,1)}, u32[]{:S(2)}) copy-start(bf16[4,32,32,128]{3,2,1,0:T(8,128)(2,1)} %param.5) | copy-start | bytes 3145732
  25.5 7.3 %collective-permute-start.3 = (bf16[32,32,128]{2,1,0:T(8,128)(2,1)S(1)}, bf16[32,32,128]{2,1,0:T(8,128)(2,1)S(1)}, u32[]{:S(2)}, u32[]{:S(2)}) collective-permute-start(bf16[32,32,128]{2,1,0:T(8,128)(2,1)S(1)} %get-tuple-element.30), channel_id=1, source_target_pairs={{1,0},{2,1},{3,2},{4,3},{5,4},{6,5},{7,6},{8,7},{9,8},{10,9},{11,1... | collective-permute-start | bytes 786440 | tf_op jit(solution)/shard_map/ppermute | solution.py:390
  26.8 6.9 %collective-permute-start.2 = (bf16[32,32,128]{2,1,0:T(8,128)(2,1)S(1)}, bf16[32,32,128]{2,1,0:T(8,128)(2,1)S(1)}, u32[]{:S(2)}, u32[]{:S(2)}) collective-permute-start(bf16[32,32,128]{2,1,0:T(8,128)(2,1)S(1)} %get-tuple-element.30), channel_id=1, source_target_pairs={{0,1},{1,2},{2,3},{3,4},{4,5},{5,6},{6,7},{7,8},{8,9},{9,10},{10,1... | collective-permute-start | bytes 786440 | tf_op jit(solution)/shard_map/ppermute | solution.py:390
